TPU v7x, 512 devices: a whole 4x8x8 slice. The times are simulated.
512 devices in a mesh: pipe: 16 (over z, core), expert: 32 (over y, x).
Axes of the slice: x: 4, y: 8, z: 8, core: 2. Of those that a mesh axis runs over, the one named last changes fastest.
Arguments:
- fwd_state: bfloat16 [16, 768, 3584], P('pipe', 'expert'), may hold values from -6 to 6
- bwd_state: bfloat16 [16, 768, 3584], P('pipe', 'expert'), may hold values from -6 to 6
- saved_input: bfloat16 [16, 2, 768, 3584], P('pipe', None, 'expert'), may hold values from -6 to 6
- fwd_route: int32 [16, 2, 768, 1], P('pipe', None, 'expert'), may hold values from 0 to 3; in each aligned block of 24 rows (0 to 23, 24 to 47, ..., all dimensions but the last counted through in order) at most 7 rows name the same one
- bwd_route: int32 [16, 2, 768, 1], P('pipe', None, 'expert'), may hold values from 0 to 3; in each aligned block of 24 rows (0 to 23, 24 to 47, ..., all dimensions but the last counted through in order) at most 7 rows name the same one
- fwd_gate: float32 [16, 2, 768], P('pipe', None, 'expert'), may hold values from 0.3 to 1
- bwd_gate: float32 [16, 2, 768], P('pipe', None, 'expert'), may hold values from 0.3 to 1
- w_gate: bfloat16 [16, 3584, 4096], P('pipe', None, 'expert'), may hold values from -0.09375 to 0.09375
- w_up: bfloat16 [16, 3584, 4096], P('pipe', None, 'expert'), may hold values from -0.09375 to 0.09375
- w_down: bfloat16 [16, 4096, 3584], P('pipe', 'expert'), may hold values from -0.1875 to 0.1875
- norm_gain: float32 [16, 3584], P('pipe'), may hold values from 0.5 to 1.5
Outputs:
- fwd_out: bfloat16 [16, 768, 3584], P('pipe', 'expert')
- bwd_out: bfloat16 [16, 768, 3584], P('pipe', 'expert')
Inputs may be any that keep to these rules, and one draw needn't show every extreme that they name: `fwd_route`: in the rows of one device at one rank and step, no expert is named more than 7 times, and one is named exactly 7 times. `bwd_route`: as for fwd_route.
All inputs are finite; a program needn't handle non-finite values.
Results may differ from a plain program's by a relative error of at most 0.0068.
Values may be sent and summed in bfloat16 or wider, within the bound.
A program may use at most 64 MiB of HBM per device.

v0:
```python
import jax
import jax.numpy as jnp
from jax import lax
from jax.sharding import PartitionSpec as P

EXPERTS = 4
CAP = 7


EPS = 1e-06


def passed_along(array, axis, by):
    size = lax.axis_size(axis)
    pairs = [(i, i + by) for i in range(size) if 0 <= i + by < size]
    return lax.ppermute(array, axis, pairs)


def norm_rows(rows, gain):
    raw = rows.astype(jnp.float32)
    scale = lax.rsqrt(jnp.mean(raw * raw, axis=-1, keepdims=True) + EPS)
    return (raw, scale, (raw * scale * gain).astype(jnp.bfloat16))


def slot_index(route):
    hits = (route[:, None] == jnp.arange(EXPERTS, dtype=jnp.int32)[None, :]).astype(jnp.int32)
    before = jnp.cumsum(hits, axis=0) - hits
    return route * CAP + jnp.sum(before * hits, axis=1)


def slot_table(index):
    columns = jnp.arange(EXPERTS * CAP, dtype=jnp.int32)
    return (columns[:, None] == index[None, :]).astype(jnp.bfloat16)


def fill_slots(table, rows, shards):
    picked = jnp.dot(table, rows, preferred_element_type=jnp.float32).astype(jnp.bfloat16)
    return jnp.repeat(picked.reshape(EXPERTS, CAP, rows.shape[1]), shards, axis=0)


def collect_rows(returned, index, shards):
    width = returned.shape[2]
    summed = (
        returned.reshape(EXPERTS, shards, returned.shape[1], width).astype(jnp.float32).sum(axis=1)
    )
    return jnp.take(summed.reshape(EXPERTS * CAP, width), index, axis=0)


def local(
    fwd_state,
    bwd_state,
    saved_input,
    fwd_route,
    bwd_route,
    fwd_gate,
    bwd_gate,
    w_gate,
    w_up,
    w_down,
    norm_gain,
):
    shards = lax.axis_size("expert") // EXPERTS
    gain = norm_gain[0]
    gate_cols = w_gate[0]
    up_cols = w_up[0]
    down_rows = w_down[0]
    steps_total = fwd_route.shape[1]
    forward = fwd_state[0]
    backward = bwd_state[0]
    new_forward = forward
    new_backward = backward
    for moment in range(steps_total):
        fwd_index = slot_index(fwd_route[0, moment, :, 0])
        fwd_raw, fwd_scale, fwd_norm = norm_rows(forward, gain)
        fwd_slots = fill_slots(slot_table(fwd_index), fwd_norm, shards)
        bwd_index = slot_index(bwd_route[0, moment, :, 0])
        bwd_table = slot_table(bwd_index)
        bwd_raw, bwd_scale, bwd_norm = norm_rows(saved_input[0, moment], gain)
        scaled = (bwd_gate[0, moment][:, None] * backward.astype(jnp.float32)).astype(jnp.bfloat16)
        bwd_inputs = fill_slots(bwd_table, bwd_norm, shards)
        bwd_grads = fill_slots(bwd_table, scaled, shards)
        expert_received = lax.all_to_all(
            fwd_slots, "expert", split_axis=0, concat_axis=0, tiled=True
        )
        expert_gated = jnp.einsum(
            "scd,dh->sch", expert_received, gate_cols, preferred_element_type=jnp.float32
        )
        expert_upped = jnp.einsum(
            "scd,dh->sch", expert_received, up_cols, preferred_element_type=jnp.float32
        )
        hidden = (expert_gated * jax.nn.sigmoid(expert_gated) * expert_upped).astype(jnp.bfloat16)
        fwd_partial = jnp.einsum(
            "sch,hd->scd", hidden, down_rows, preferred_element_type=jnp.float32
        ).astype(jnp.bfloat16)
        fwd_back = lax.all_to_all(fwd_partial, "expert", split_axis=0, concat_axis=0, tiled=True)
        inputs_part = lax.all_to_all(bwd_inputs, "expert", split_axis=0, concat_axis=0, tiled=True)
        grads_part = lax.all_to_all(bwd_grads, "expert", split_axis=0, concat_axis=0, tiled=True)
        gated = jnp.einsum(
            "scd,dh->sch", inputs_part, gate_cols, preferred_element_type=jnp.float32
        )
        upped = jnp.einsum("scd,dh->sch", inputs_part, up_cols, preferred_element_type=jnp.float32)
        dhidden = jnp.einsum(
            "scd,hd->sch", grads_part, down_rows, preferred_element_type=jnp.float32
        )
        sigma = jax.nn.sigmoid(gated)
        dgate = (dhidden * upped * sigma * (1.0 + gated * (1.0 - sigma))).astype(jnp.bfloat16)
        dup = (dhidden * gated * sigma).astype(jnp.bfloat16)
        result = jnp.einsum("sch,dh->scd", dgate, gate_cols, preferred_element_type=jnp.float32)
        result = result + jnp.einsum(
            "sch,dh->scd", dup, up_cols, preferred_element_type=jnp.float32
        )
        bwd_partial = result.astype(jnp.bfloat16)
        bwd_back = lax.all_to_all(bwd_partial, "expert", split_axis=0, concat_axis=0, tiled=True)
        moe_rows = collect_rows(fwd_back, fwd_index, shards)
        new_forward = (fwd_raw + fwd_gate[0, moment][:, None] * moe_rows).astype(jnp.bfloat16)
        dnorm = collect_rows(bwd_back, bwd_index, shards)
        weighted = gain * dnorm
        cubed = bwd_scale * bwd_scale * bwd_scale
        dinput = bwd_scale * weighted - bwd_raw * cubed * jnp.mean(
            bwd_raw * weighted, axis=-1, keepdims=True
        )
        new_backward = (backward.astype(jnp.float32) + dinput).astype(jnp.bfloat16)
        if moment + 1 < steps_total:
            forward = passed_along(new_forward, "pipe", 1)
            backward = passed_along(new_backward, "pipe", -1)
    return (new_forward[None], new_backward[None])


def solution(mesh):
    placed = (
        P("pipe", "expert", None),
        P("pipe", "expert", None),
        P("pipe", None, "expert", None),
        P("pipe", None, "expert", None),
        P("pipe", None, "expert", None),
        P("pipe", None, "expert"),
        P("pipe", None, "expert"),
        P("pipe", None, "expert"),
        P("pipe", None, "expert"),
        P("pipe", "expert", None),
        P("pipe", None),
    )
    return jax.shard_map(
        local,
        mesh=mesh,
        in_specs=placed,
        out_specs=(P("pipe", "expert", None), P("pipe", "expert", None)),
        check_vma=False,
    )
```

profile of v0, /device:TPU:272, one launch (start us, length us, event | category | flops | bytes accessed | tf_op | source)
XLA Modules:
  0.0 510.9 jit_solution(14724402480912951104)
XLA Ops:
  7.0 10.2 %all-to-all-start.4 = ((bf16[32,7,3584]{2,1,0:T(8,128)(2,1)}), bf16[32,7,3584]{2,1,0:T(8,128)(2,1)S(1)}, u32[]{:S(2)}, u32[]{:S(2)}) async-start(bf16[32,7,3584]{2,1,0:T(8,128)(2,1)} %bitcast.22), calls=%async_computation.4 | async-start | bytes 3670016 | tf_op jit(solution)/shard_map/all_to_all | solution.py:97
  19.1 42.8 %all-to-all-done.4 = bf16[32,7,3584]{2,1,0:T(8,128)(2,1)S(1)} async-done(((bf16[32,7,3584]{2,1,0:T(8,128)(2,1)}), bf16[32,7,3584]{2,1,0:T(8,128)(2,1)S(1)}, u32[]{:S(2)}, u32[]{:S(2)}) %all-to-all-start.4) | async-done | bytes 1605664 | tf_op jit(solution)/shard_map/all_to_all | solution.py:97
  64.4 6.0 %all-to-all-start.5 = ((bf16[32,7,3584]{2,1,0:T(8,128)(2,1)}), bf16[32,7,3584]{2,1,0:T(8,128)(2,1)S(1)}, u32[]{:S(2)}, u32[]{:S(2)}) async-start(bf16[32,7,3584]{2,1,0:T(8,128)(2,1)} %bitcast.24), calls=%async_computation.5 | async-start | bytes 3670016 | tf_op jit(solution)/shard_map/all_to_all | solution.py:96
  72.6 41.2 %all-to-all-done.5 = bf16[32,7,3584]{2,1,0:T(8,128)(2,1)S(1)} async-done(((bf16[32,7,3584]{2,1,0:T(8,128)(2,1)}), bf16[32,7,3584]{2,1,0:T(8,128)(2,1)S(1)}, u32[]{:S(2)}, u32[]{:S(2)}) %all-to-all-start.5) | async-done | bytes 1605664 | tf_op jit(solution)/shard_map/all_to_all | solution.py:96
  113.8 2.5 broadcast_in_dim.25
  116.4 5.7 %all-to-all-start = ((bf16[32,7,3584]{2,1,0:T(8,128)(2,1)}), bf16[32,7,3584]{2,1,0:T(8,128)(2,1)S(1)}, u32[]{:S(2)}, u32[]{:S(2)}) async-start(bf16[32,7,3584]{2,1,0:T(8,128)(2,1)} %bitcast.4), calls=%async_computation | async-start | bytes 3670016 | tf_op jit(solution)/shard_map/all_to_all | solution.py:82
  122.1 2.6 fusion.4
  125.5 4.7 fusion.66
  134.9 29.7 %all-to-all-done = bf16[32,7,3584]{2,1,0:T(8,128)(2,1)S(1)} async-done(((bf16[32,7,3584]{2,1,0:T(8,128)(2,1)}), bf16[32,7,3584]{2,1,0:T(8,128)(2,1)S(1)}, u32[]{:S(2)}, u32[]{:S(2)}) %all-to-all-start) | async-done | bytes 1605664 | tf_op jit(solution)/shard_map/all_to_all | solution.py:82
  165.9 5.7 %all-to-all-start.6 = ((bf16[32,7,3584]{2,1,0:T(8,128)(2,1)}), bf16[32,7,3584]{2,1,0:T(8,128)(2,1)S(1)}, u32[]{:S(2)}, u32[]{:S(2)}) async-start(bf16[32,7,3584]{2,1,0:T(8,128)(2,1)} %copy.38), calls=%async_computation.6 | async-start | bytes 3670016 | tf_op jit(solution)/shard_map/all_to_all | solution.py:113
  174.2 4.2 convolution_convert_fusion.1
  178.3 3.6 copy.27
  181.9 31.9 %all-to-all-done.6 = bf16[32,7,3584]{2,1,0:T(8,128)(2,1)S(1)} async-done(((bf16[32,7,3584]{2,1,0:T(8,128)(2,1)}), bf16[32,7,3584]{2,1,0:T(8,128)(2,1)S(1)}, u32[]{:S(2)}, u32[]{:S(2)}) %all-to-all-start.6) | async-done | bytes 1605664 | tf_op jit(solution)/shard_map/all_to_all | solution.py:113
  215.0 5.7 %all-to-all-start.1 = ((bf16[32,7,3584]{2,1,0:T(8,128)(2,1)}), bf16[32,7,3584]{2,1,0:T(8,128)(2,1)S(1)}, u32[]{:S(2)}, u32[]{:S(2)}) async-start(bf16[32,7,3584]{2,1,0:T(8,128)(2,1)} %copy.27), calls=%async_computation.1 | async-start | bytes 3670016 | tf_op jit(solution)/shard_map/all_to_all | solution.py:95
  221.3 2.7 convert_reduce_fusion.1
  230.6 31.8 %all-to-all-done.1 = bf16[32,7,3584]{2,1,0:T(8,128)(2,1)S(1)} async-done(((bf16[32,7,3584]{2,1,0:T(8,128)(2,1)}), bf16[32,7,3584]{2,1,0:T(8,128)(2,1)S(1)}, u32[]{:S(2)}, u32[]{:S(2)}) %all-to-all-start.1) | async-done | bytes 1605664 | tf_op jit(solution)/shard_map/all_to_all | solution.py:95
  263.8 5.3 %all-to-all-start.8 = ((bf16[32,7,3584]{2,1,0:T(8,128)(2,1)}), bf16[32,7,3584]{2,1,0:T(8,128)(2,1)}, u32[]{:S(2)}, u32[]{:S(2)}) async-start(bf16[32,7,3584]{2,1,0:T(8,128)(2,1)} %bitcast.125), calls=%async_computation.8 | async-start | bytes 3670016 | tf_op jit(solution)/shard_map/all_to_all | solution.py:96
  273.7 6.0 %collective-permute-done = bf16[24,3584]{1,0:T(8,128)(2,1)S(1)} collective-permute-done((bf16[24,3584]{1,0:T(8,128)(2,1)S(1)}, bf16[24,3584]{1,0:T(8,128)(2,1)S(1)}, u32[]{:S(2)}, u32[]{:S(2)}) %collective-permute-start) | collective-permute-done | bytes 172064 | tf_op jit(solution)/shard_map/ppermute | solution.py:16
  280.8 30.8 %all-to-all-done.8 = bf16[32,7,3584]{2,1,0:T(8,128)(2,1)} async-done(((bf16[32,7,3584]{2,1,0:T(8,128)(2,1)}), bf16[32,7,3584]{2,1,0:T(8,128)(2,1)}, u32[]{:S(2)}, u32[]{:S(2)}) %all-to-all-start.8) | async-done | bytes 1605664 | tf_op jit(solution)/shard_map/all_to_all | solution.py:96
  312.9 5.9 %all-to-all-start.2 = ((bf16[32,7,3584]{2,1,0:T(8,128)(2,1)}), bf16[32,7,3584]{2,1,0:T(8,128)(2,1)S(1)}, u32[]{:S(2)}, u32[]{:S(2)}) async-start(bf16[32,7,3584]{2,1,0:T(8,128)(2,1)} %bitcast.14), calls=%async_computation.2 | async-start | bytes 3670016 | tf_op jit(solution)/shard_map/all_to_all | solution.py:82
  321.9 2.9 collective-permute-done.1
  325.8 35.0 %all-to-all-done.2 = bf16[32,7,3584]{2,1,0:T(8,128)(2,1)S(1)} async-done(((bf16[32,7,3584]{2,1,0:T(8,128)(2,1)}), bf16[32,7,3584]{2,1,0:T(8,128)(2,1)S(1)}, u32[]{:S(2)}, u32[]{:S(2)}) %all-to-all-start.2) | async-done | bytes 1605664 | tf_op jit(solution)/shard_map/all_to_all | solution.py:82
  362.2 5.8 %all-to-all-start.7 = ((bf16[32,7,3584]{2,1,0:T(8,128)(2,1)}), bf16[32,7,3584]{2,1,0:T(8,128)(2,1)}, u32[]{:S(2)}, u32[]{:S(2)}) async-start(bf16[32,7,3584]{2,1,0:T(8,128)(2,1)} %bitcast.29), calls=%async_computation.7 | async-start | bytes 3670016 | tf_op jit(solution)/shard_map/all_to_all | solution.py:97
  369.9 3.7 convolution_convert_fusion
  373.6 3.5 copy.32
  377.1 32.6 %all-to-all-done.7 = bf16[32,7,3584]{2,1,0:T(8,128)(2,1)} async-done(((bf16[32,7,3584]{2,1,0:T(8,128)(2,1)}), bf16[32,7,3584]{2,1,0:T(8,128)(2,1)}, u32[]{:S(2)}, u32[]{:S(2)}) %all-to-all-start.7) | async-done | bytes 1605664 | tf_op jit(solution)/shard_map/all_to_all | solution.py:97
  409.8 5.2 %all-to-all-start.3 = ((bf16[32,7,3584]{2,1,0:T(8,128)(2,1)}), bf16[32,7,3584]{2,1,0:T(8,128)(2,1)S(1)}, u32[]{:S(2)}, u32[]{:S(2)}) async-start(bf16[32,7,3584]{2,1,0:T(8,128)(2,1)} %copy.32), calls=%async_computation.3 | async-start | bytes 3670016 | tf_op jit(solution)/shard_map/all_to_all | solution.py:95
  414.9 2.6 fusion.6
  419.8 4.7 fusion.63
  429.1 28.2 %all-to-all-done.3 = bf16[32,7,3584]{2,1,0:T(8,128)(2,1)S(1)} async-done(((bf16[32,7,3584]{2,1,0:T(8,128)(2,1)}), bf16[32,7,3584]{2,1,0:T(8,128)(2,1)S(1)}, u32[]{:S(2)}, u32[]{:S(2)}) %all-to-all-start.3) | async-done | bytes 1605664 | tf_op jit(solution)/shard_map/all_to_all | solution.py:95
  457.3 5.8 %all-to-all-start.9 = ((bf16[32,7,3584]{2,1,0:T(8,128)(2,1)}), bf16[32,7,3584]{2,1,0:T(8,128)(2,1)}, u32[]{:S(2)}, u32[]{:S(2)}) async-start(bf16[32,7,3584]{2,1,0:T(8,128)(2,1)} %copy.44), calls=%async_computation.9 | async-start | bytes 3670016 | tf_op jit(solution)/shard_map/all_to_all | solution.py:113
  464.7 40.4 %all-to-all-done.9 = bf16[32,7,3584]{2,1,0:T(8,128)(2,1)} async-done(((bf16[32,7,3584]{2,1,0:T(8,128)(2,1)}), bf16[32,7,3584]{2,1,0:T(8,128)(2,1)}, u32[]{:S(2)}, u32[]{:S(2)}) %all-to-all-start.9) | async-done | bytes 1605664 | tf_op jit(solution)/shard_map/all_to_all | solution.py:113
  (162 shorter events, 60.2 us)
Async XLA Ops:
  0.6 124.9 %copy-start = (bf16[1,3584,128]{2,1,0:T(8,128)(2,1)S(1)}, bf16[1,3584,128]{2,1,0:T(8,128)(2,1)}, u32[]{:S(2)}) copy-start(bf16[1,3584,128]{2,1,0:T(8,128)(2,1)} %param.21) | copy-start | bytes 2752516
  7.0 10.2 %copy-start.19 = (f32[1,3584]{1,0:T(1,128)S(1)}, f32[1,3584]{1,0:T(1,128)}, u32[]{:S(2)}) copy-start(f32[1,3584]{1,0:T(1,128)} %param.23) | copy-start | bytes 43012
  7.0 10.3 %copy-start.5 = (bf16[1,2,24,3584]{3,2,1,0:T(8,128)(2,1)S(1)}, bf16[1,2,24,3584]{3,2,1,0:T(8,128)(2,1)}, u32[]{:S(2)}) copy-start(bf16[1,2,24,3584]{3,2,1,0:T(8,128)(2,1)} %param.15) | copy-start | bytes 1032196
  7.0 54.8 %all-to-all-start.4 = ((bf16[32,7,3584]{2,1,0:T(8,128)(2,1)}), bf16[32,7,3584]{2,1,0:T(8,128)(2,1)S(1)}, u32[]{:S(2)}, u32[]{:S(2)}) async-start(bf16[32,7,3584]{2,1,0:T(8,128)(2,1)} %bitcast.22), calls=%async_computation.4 | async-start | bytes 3670016 | tf_op jit(solution)/shard_map/all_to_all | solution.py:97
  17.3 54.3 %copy-start.14 = (f32[3584]{0:T(1024)}, f32[3584]{0:T(1024)S(1)}, u32[]{:S(2)}) copy-start(f32[3584]{0:T(1024)S(1)} %reduce) | copy-start | bytes 43012
  18.0 46.3 %copy-start.30 = (f32[24]{0:T(128)}, f32[24]{0:T(128)S(1)}, u32[]{:S(2)}) copy-start(f32[24]{0:T(128)S(1)} %get-tuple-element.28) | copy-start | bytes 292
  64.4 6.0 %copy-start.24 = (s32[1,2,24,1]{2,3,1,0:T(1,128)S(1)}, s32[1,2,24,1]{2,3,1,0:T(1,128)}, u32[]{:S(2)}) copy-start(s32[1,2,24,1]{2,3,1,0:T(1,128)} %param.16) | copy-start | bytes 580
  64.4 6.4 %copy-start.12 = (bf16[1,24,3584]{2,1,0:T(8,128)(2,1)S(1)}, bf16[1,24,3584]{2,1,0:T(8,128)(2,1)}, u32[]{:S(2)}) copy-start(bf16[1,24,3584]{2,1,0:T(8,128)(2,1)} %param.13) | copy-start | bytes 516100
  64.4 49.5 %all-to-all-start.5 = ((bf16[32,7,3584]{2,1,0:T(8,128)(2,1)}), bf16[32,7,3584]{2,1,0:T(8,128)(2,1)S(1)}, u32[]{:S(2)}, u32[]{:S(2)}) async-start(bf16[32,7,3584]{2,1,0:T(8,128)(2,1)} %bitcast.24), calls=%async_computation.5 | async-start | bytes 3670016 | tf_op jit(solution)/shard_map/all_to_all | solution.py:96
  71.5 44.8 %copy-start.28 = (s32[24]{0:T(128)}, s32[24]{0:T(128)S(1)}, u32[]{:S(2)}) copy-start(s32[24]{0:T(128)S(1)} %get-tuple-element.22) | copy-start | bytes 292
  116.4 48.3 %all-to-all-start = ((bf16[32,7,3584]{2,1,0:T(8,128)(2,1)}), bf16[32,7,3584]{2,1,0:T(8,128)(2,1)S(1)}, u32[]{:S(2)}, u32[]{:S(2)}) async-start(bf16[32,7,3584]{2,1,0:T(8,128)(2,1)} %bitcast.4), calls=%async_computation | async-start | bytes 3670016 | tf_op jit(solution)/shard_map/all_to_all | solution.py:82
  165.9 47.9 %all-to-all-start.6 = ((bf16[32,7,3584]{2,1,0:T(8,128)(2,1)}), bf16[32,7,3584]{2,1,0:T(8,128)(2,1)S(1)}, u32[]{:S(2)}, u32[]{:S(2)}) async-start(bf16[32,7,3584]{2,1,0:T(8,128)(2,1)} %copy.38), calls=%async_computation.6 | async-start | bytes 3670016 | tf_op jit(solution)/shard_map/all_to_all | solution.py:113
  215.0 47.5 %all-to-all-start.1 = ((bf16[32,7,3584]{2,1,0:T(8,128)(2,1)}), bf16[32,7,3584]{2,1,0:T(8,128)(2,1)S(1)}, u32[]{:S(2)}, u32[]{:S(2)}) async-start(bf16[32,7,3584]{2,1,0:T(8,128)(2,1)} %copy.27), calls=%async_computation.1 | async-start | bytes 3670016 | tf_op jit(solution)/shard_map/all_to_all | solution.py:95
  263.8 6.0 %copy-start.38 = (f32[1,2,24]{2,1,0:T(2,128)S(1)}, f32[1,2,24]{2,1,0:T(2,128)}, u32[]{:S(2)}) copy-start(f32[1,2,24]{2,1,0:T(2,128)} %param.18) | copy-start | bytes 580
  263.8 47.7 %all-to-all-start.8 = ((bf16[32,7,3584]{2,1,0:T(8,128)(2,1)}), bf16[32,7,3584]{2,1,0:T(8,128)(2,1)}, u32[]{:S(2)}, u32[]{:S(2)}) async-start(bf16[32,7,3584]{2,1,0:T(8,128)(2,1)} %bitcast.125), calls=%async_computation.8 | async-start | bytes 3670016 | tf_op jit(solution)/shard_map/all_to_all | solution.py:96
  270.8 9.6 %copy-start.15 = (f32[3584]{0:T(1024)S(1)}, f32[3584]{0:T(1024)}, u32[]{:S(2)}) copy-start(f32[3584]{0:T(1024)} %copy-done.14) | copy-start | bytes 43012
  270.8 9.6 %copy-start.26 = (s32[24]{0:T(128)S(1)}, s32[24]{0:T(128)}, u32[]{:S(2)}) copy-start(s32[24]{0:T(128)} %get-tuple-element.10) | copy-start | bytes 292
  271.8 7.9 %collective-permute-start = (bf16[24,3584]{1,0:T(8,128)(2,1)S(1)}, bf16[24,3584]{1,0:T(8,128)(2,1)S(1)}, u32[]{:S(2)}, u32[]{:S(2)}) collective-permute-start(bf16[24,3584]{1,0:T(8,128)(2,1)S(1)} %fusion.99), channel_id=1, source_target_pairs={{0,32},{32,64},{64,96},{96,128},{128,160},{160,192},{192,224},{224... | collective-permute-start | bytes 516104 | tf_op jit(solution)/shard_map/ppermute | solution.py:16
  312.9 5.9 %copy-start.39 = (f32[24]{0:T(128)S(1)}, f32[24]{0:T(128)}, u32[]{:S(2)}) copy-start(f32[24]{0:T(128)} %get-tuple-element.4) | copy-start | bytes 292
  312.9 6.0 %copy-start.8 = (f32[24,3584]{1,0:T(8,128)S(1)}, f32[24,3584]{1,0:T(8,128)}, u32[]{:S(2)}) copy-start(f32[24,3584]{1,0:T(8,128)} %gather_fusion.2) | copy-start | bytes 1032196
  312.9 6.0 %copy-start.22 = (pred[24]{0:T(512)(128)(4,1)S(1)}, pred[24]{0:T(512)(128)(4,1)}, u32[]{:S(2)}) copy-start(pred[24]{0:T(512)(128)(4,1)} %get-tuple-element.13) | copy-start | bytes 76
  312.9 6.0 %copy-start.31 = (f32[24]{0:T(128)S(1)}, f32[24]{0:T(128)}, u32[]{:S(2)}) copy-start(f32[24]{0:T(128)} %copy-done.30) | copy-start | bytes 292
  312.9 6.0 %copy-start.40 = (f32[24]{0:T(128)S(1)}, f32[24]{0:T(128)}, u32[]{:S(2)}) copy-start(f32[24]{0:T(128)} %get-tuple-element.27) | copy-start | bytes 292
  312.9 12.6 %copy-start.20 = (s32[24]{0:T(128)S(1)}, s32[24]{0:T(128)}, u32[]{:S(2)}) copy-start(s32[24]{0:T(128)} %get-tuple-element.6) | copy-start | bytes 292
  312.9 12.6 %copy-start.25 = (f32[24]{0:T(128)S(1)}, f32[24]{0:T(128)}, u32[]{:S(2)}) copy-start(f32[24]{0:T(128)} %get-tuple-element.17) | copy-start | bytes 292
  312.9 47.9 %all-to-all-start.2 = ((bf16[32,7,3584]{2,1,0:T(8,128)(2,1)}), bf16[32,7,3584]{2,1,0:T(8,128)(2,1)S(1)}, u32[]{:S(2)}, u32[]{:S(2)}) async-start(bf16[32,7,3584]{2,1,0:T(8,128)(2,1)} %bitcast.14), calls=%async_computation.2 | async-start | bytes 3670016 | tf_op jit(solution)/shard_map/all_to_all | solution.py:82
  320.0 4.8 collective-permute-start.1
  362.2 47.6 %all-to-all-start.7 = ((bf16[32,7,3584]{2,1,0:T(8,128)(2,1)}), bf16[32,7,3584]{2,1,0:T(8,128)(2,1)}, u32[]{:S(2)}, u32[]{:S(2)}) async-start(bf16[32,7,3584]{2,1,0:T(8,128)(2,1)} %bitcast.29), calls=%async_computation.7 | async-start | bytes 3670016 | tf_op jit(solution)/shard_map/all_to_all | solution.py:97
  409.8 47.5 %all-to-all-start.3 = ((bf16[32,7,3584]{2,1,0:T(8,128)(2,1)}), bf16[32,7,3584]{2,1,0:T(8,128)(2,1)S(1)}, u32[]{:S(2)}, u32[]{:S(2)}) async-start(bf16[32,7,3584]{2,1,0:T(8,128)(2,1)} %copy.32), calls=%async_computation.3 | async-start | bytes 3670016 | tf_op jit(solution)/shard_map/all_to_all | solution.py:95
  429.1 34.0 %copy-start.27 = (s32[24]{0:T(128)S(1)}, s32[24]{0:T(128)}, u32[]{:S(2)}) copy-start(s32[24]{0:T(128)} %get-tuple-element.10) | copy-start | bytes 292
  429.1 34.6 %copy-start.21 = (s32[24]{0:T(128)S(1)}, s32[24]{0:T(128)}, u32[]{:S(2)}) copy-start(s32[24]{0:T(128)} %get-tuple-element.6) | copy-start | bytes 292
  457.3 47.9 %all-to-all-start.9 = ((bf16[32,7,3584]{2,1,0:T(8,128)(2,1)}), bf16[32,7,3584]{2,1,0:T(8,128)(2,1)}, u32[]{:S(2)}, u32[]{:S(2)}) async-start(bf16[32,7,3584]{2,1,0:T(8,128)(2,1)} %copy.44), calls=%async_computation.9 | async-start | bytes 3670016 | tf_op jit(solution)/shard_map/all_to_all | solution.py:113
  (22 other events, 36.5 us)
where the time goes:
time: 513 us; the launch traced here: 511 us
  waiting for transfers between devices  353 us (69%)
  starting transfers between devices  65.2 us (13%)
  matrix products  38.1 us (7%)
  local copies, waits for them, and re-layouts  36 us (7%)
  other arithmetic  17 us (3%)
    all_to_all x2, waiting for transfers between devices, local(): lax.all_to_all(bwd_grads, 'expert', split_axis=0, concat_axis=0, tiled=True)  75.4 us
    all_to_all x2, waiting for transfers between devices, local(): lax.all_to_all(bwd_partial, 'expert', split_axis=0, concat_axis=0, tiled=...  72.3 us
    all_to_all x2, waiting for transfers between devices, local(): lax.all_to_all(bwd_inputs, 'expert', split_axis=0, concat_axis=0, tiled=T...  72 us
    all_to_all x2, waiting for transfers between devices, local(): lax.all_to_all(fwd_slots, 'expert', split_axis=0, concat_axis=0, tiled=True)  64.7 us
    all_to_all x2, waiting for transfers between devices, local(): lax.all_to_all(fwd_partial, 'expert', split_axis=0, concat_axis=0, tiled=...  59.9 us
    all_to_all x2, starting transfers between devices, local(): lax.all_to_all(bwd_grads, 'expert', split_axis=0, concat_axis=0, tiled=True)  16 us
    all_to_all x2, starting transfers between devices, local(): lax.all_to_all(fwd_slots, 'expert', split_axis=0, concat_axis=0, tiled=True)  11.6 us
    all_to_all x2, starting transfers between devices, local(): lax.all_to_all(bwd_partial, 'expert', split_axis=0, concat_axis=0, tiled=...  11.5 us
  transfers between devices with their start and end apart: 12, of which 12 were waited for; matrix products, arithmetic and copies ran while one was open for 13% of the time, Pallas kernels for 0%

commit v1 on v0

v1 whole, which is shorter than its diff:
```python
import functools

import jax
import jax.numpy as jnp
from jax import lax
from jax.experimental import pallas as pl
from jax.experimental.pallas import tpu as pltpu
from jax.sharding import PartitionSpec as P

EPS = 1e-06
NX = 4
PAIR = 2
SLOT = 8
BLK = 2 * SLOT
NT = (((1,), (1,)), ((), ()))


def dot(a, b):
    return jnp.dot(a, b, preferred_element_type=jnp.float32)


def dot_nt(a, b):
    return lax.dot_general(a, b, NT, preferred_element_type=jnp.float32)


def slots_of(route):
    tok = route.shape[0]
    lane = lax.broadcasted_iota(jnp.int32, (tok, 128), 1)
    hits = jnp.where(lane == route, 1.0, 0.0)
    row_i = lax.broadcasted_iota(jnp.int32, (tok, tok), 0)
    col_i = lax.broadcasted_iota(jnp.int32, (tok, tok), 1)
    lower = jnp.where(col_i < row_i, 1.0, 0.0)
    before = dot(lower.astype(jnp.bfloat16), hits.astype(jnp.bfloat16))
    return jnp.sum(before * hits, axis=1, keepdims=True).astype(jnp.int32)


def as_row(col):
    tok = col.shape[0]
    row_i = lax.broadcasted_iota(jnp.int32, (tok, tok), 0)
    col_i = lax.broadcasted_iota(jnp.int32, (tok, tok), 1)
    return jnp.sum(jnp.where(row_i == col_i, col, 0), axis=0, keepdims=True)


def as_col(row):
    tok = row.shape[1]
    row_i = lax.broadcasted_iota(jnp.int32, (tok, tok), 0)
    col_i = lax.broadcasted_iota(jnp.int32, (tok, tok), 1)
    return jnp.sum(jnp.where(row_i == col_i, row, 0.0), axis=1, keepdims=True)


def place(route, slot, rows, shift):
    target = as_row(route * BLK + (slot + shift))
    sub = lax.broadcasted_iota(jnp.int32, (rows, route.shape[0]), 0)
    return jnp.where(sub == target, 1.0, 0.0).astype(jnp.bfloat16)


def pick(route, slot, ny, shift):
    lane = lax.broadcasted_iota(jnp.int32, (route.shape[0], ny * BLK), 1)
    mine = (lane % BLK == slot + shift) & (lane // (BLK * PAIR) == route)
    return jnp.where(mine, 1.0, 0.0).astype(jnp.bfloat16)


def kernel(
    ny, npipe, ct,
    fs, bs, sv, fr, br, fg, bg, gain, wg, wu, wd,
    fo, bo,
    wgu, wdn, mb, m0, m1, nrm, sca, dd, d1, gs, gs1, dh, hs, ab, r0s, r0r, r1s, r1r,
    dn, xf, xb, yf, yb,
    l_sem, ws_sem, wr_sem, ds_sem, dr_sem, rs_sem, rr_sem, ss_sem, sr_sem,
):
    width = wd.shape[1]
    hid = wd.shape[0]
    tok = fs.shape[0]
    tiles = width // ct
    me = lax.axis_index("expert")
    pipe = lax.axis_index("pipe")
    y, x = me // NX, me % NX
    right = y * NX + (x + 1) % NX
    left = y * NX + (x + NX - 1) % NX
    p_next = (pipe + 1) % npipe
    p_prev = (pipe + npipe - 1) % npipe
    mesh_id = pl.DeviceIdType.MESH

    def row_dev(k):
        return ((y + k) % ny) * NX + x

    loads = [
        pltpu.make_async_copy(wg, wgu.at[0, :, pl.ds(0, hid)], l_sem.at[0]),
        pltpu.make_async_copy(wu, wgu.at[0, :, pl.ds(hid, hid)], l_sem.at[1]),
        pltpu.make_async_copy(wd, wdn.at[pl.ds(0, hid)], l_sem.at[2]),
    ]
    for c in loads:
        c.start()

    barrier = pltpu.get_barrier_semaphore()
    for k in range(1, ny):
        pl.semaphore_signal(barrier, inc=1, device_id=(pipe, row_dev(k)), device_id_type=mesh_id)
    for dev in (right, left):
        pl.semaphore_signal(barrier, inc=1, device_id=(pipe, dev), device_id_type=mesh_id)
    for q in (p_next, p_prev):
        pl.semaphore_signal(barrier, inc=1, device_id=(q, me), device_id_type=mesh_id)
    pl.semaphore_wait(barrier, ny - 1 + 4)

    def remote(src, dst, send, recv, dev):
        return pltpu.make_async_remote_copy(
            src_ref=src, dst_ref=dst, send_sem=send, recv_sem=recv,
            device_id=dev, device_id_type=mesh_id,
        )

    def w_copy(i, src, dst, dev):
        return remote(src, dst, ws_sem.at[i], wr_sem.at[i], (pipe, dev))

    half = width // 2
    hh = hid // 2
    w = [
        w_copy(0, wgu.at[0], wgu.at[1], right),
        w_copy(1, wgu.at[0], wgu.at[2], left),
        w_copy(2, wdn.at[pl.ds(0, hid)], wdn.at[pl.ds(hid, hid)], right),
        w_copy(3, wdn.at[pl.ds(0, hid)], wdn.at[pl.ds(2 * hid, hid)], left),
        w_copy(4, wgu.at[1, pl.ds(0, half)], wgu.at[3, pl.ds(0, half)], right),
        w_copy(5, wgu.at[2, pl.ds(half, half)], wgu.at[3, pl.ds(half, half)], left),
        w_copy(6, wdn.at[pl.ds(hid, hh)], wdn.at[pl.ds(3 * hid, hh)], right),
        w_copy(7, wdn.at[pl.ds(2 * hid + hh, hh)], wdn.at[pl.ds(3 * hid + hh, hh)], left),
    ]
    loads[0].wait()
    loads[1].wait()
    w[0].start()
    w[1].start()
    loads[2].wait()
    w[2].start()
    w[3].start()

    order = sorted(range(1, ny), key=lambda k: -min(k, ny - k))

    def scatter(phase, m, d, base):
        for k in order:
            e = ((y + k) % ny) // PAIR
            remote(
                m.at[pl.ds(pl.multiple_of(e * BLK, BLK), BLK)],
                d.at[pl.ds(pl.multiple_of(base + y * BLK, BLK), BLK)],
                ds_sem.at[phase, k], dr_sem.at[phase, k], (pipe, row_dev(k)),
            ).start()
        d[pl.ds(pl.multiple_of(base + y * BLK, BLK), BLK), :] = m[
            pl.ds(pl.multiple_of((y // PAIR) * BLK, BLK), BLK), :
        ]

    def scatter_wait(phase, m, d, base, recv):
        for k in order:
            c = remote(
                m.at[pl.ds(0, BLK)],
                d.at[pl.ds(pl.multiple_of(base + ((y + ny - k) % ny) * BLK, BLK), BLK)],
                ds_sem.at[phase, k], dr_sem.at[phase, k], (pipe, row_dev(k)),
            )
            if recv:
                c.wait_recv()
            else:
                c.wait_send()

    def give_back(t, rs, rr):
        for k in order:
            dst = (y + k) % ny
            remote(rs.at[dst], rr.at[y], rs_sem.at[t, k], rr_sem.at[t, k], (pipe, row_dev(k))).start()
        rr[pl.ds(y, 1)] = rs[pl.ds(y, 1)]

    def give_wait(t, rs, rr, recv):
        for k in order:
            c = remote(
                rs.at[(y + k) % ny], rr.at[(y + ny - k) % ny],
                rs_sem.at[t, k], rr_sem.at[t, k], (pipe, row_dev(k)),
            )
            if recv:
                c.wait_recv()
            else:
                c.wait_send()

    def norm_scale(raw):
        return lax.rsqrt(jnp.mean(raw * raw, axis=-1, keepdims=True) + EPS)

    g = gain[...]
    routes_f = [fr[t] for t in range(2)]
    routes_b = [br[t] for t in range(2)]
    slots_f = [slots_of(r) for r in routes_f]
    slots_b = [slots_of(r) for r in routes_b]
    gates_f = [as_col(fg[pl.ds(t, 1), :]) for t in range(2)]
    gates_b = [as_col(bg[pl.ds(t, 1), :]) for t in range(2)]
    m_rows = m0.shape[0]

    def fill(m, pa, pb):
        def tile(i, carry):
            cols = pl.ds(pl.multiple_of(i * ct, ct), ct)
            m[:, cols] = (dot(pa, nrm[:, cols]) + dot(pb, sca[:, cols])).astype(jnp.bfloat16)
            return carry

        lax.fori_loop(0, tiles, tile, 0)

    raw = fs[...].astype(jnp.float32)
    nrm[...] = (raw * norm_scale(raw) * g).astype(jnp.bfloat16)
    sca[...] = (gates_b[0] * bs[...].astype(jnp.float32)).astype(jnp.bfloat16)
    fill(
        m0,
        place(routes_f[0], slots_f[0], m_rows, 0),
        place(routes_b[0], slots_b[0], m_rows, SLOT),
    )
    scatter(0, m0, dd, 0)
    b_scale = []
    for t, dst in ((0, nrm), (1, sca)):
        raw = sv[t].astype(jnp.float32)
        scale = norm_scale(raw)
        b_scale.append(scale)
        dst[...] = (raw * scale * g).astype(jnp.bfloat16)
    fill(
        mb,
        place(routes_b[0], slots_b[0], m_rows, 0),
        place(routes_b[1], slots_b[1], m_rows, SLOT),
    )
    scatter(1, mb, dd, ny * BLK)

    scatter_wait(0, m0, dd, 0, True)
    scatter_wait(1, mb, dd, ny * BLK, True)

    def into_hidden(q):
        gs[q] = dot(dd[...], wgu[q]).reshape(2 * ny, BLK, 2 * hid)
        dh[q] = dot_nt(dd[pl.ds(0, ny * BLK)], wdn[pl.ds(q * hid, hid)]).reshape(ny, BLK, hid)

    into_hidden(0)
    w[0].wait_recv()
    w[4].start()
    w[1].wait_recv()
    w[5].start()
    w[2].wait_recv()
    w[6].start()
    w[3].wait_recv()
    w[7].start()
    into_hidden(1)
    into_hidden(2)
    for i in (4, 5, 6, 7):
        w[i].wait_recv()
    into_hidden(3)

    rows = ny * SLOT

    def expert_out(t, gf, rs):
        for q in range(NX):
            f = gf[q, pl.ds(0, ny), pl.ds(0, SLOT), :].reshape(rows, 2 * hid)
            gated, upped = f[:, :hid], f[:, hid:]
            hidden = gated * jax.nn.sigmoid(gated) * upped
            hs[:, pl.ds(q * hid, hid)] = hidden.astype(jnp.bfloat16)
            b = gs[q, pl.ds(ny, ny), pl.ds(t * SLOT, SLOT), :].reshape(rows, 2 * hid)
            gated, upped = b[:, :hid], b[:, hid:]
            dhid = dh[q, :, pl.ds(SLOT, SLOT), :].reshape(rows, hid)
            s = jax.nn.sigmoid(gated)
            da = dhid * upped * s * (1.0 + gated * (1.0 - s))
            db = dhid * gated * s
            ab[q, :, pl.ds(0, hid)] = da.astype(jnp.bfloat16)
            ab[q, :, pl.ds(hid, hid)] = db.astype(jnp.bfloat16)

        def tile(i, carry):
            cols = pl.ds(pl.multiple_of(i * ct, ct), ct)
            f = dot(hs[...], wdn[:, cols])
            b = dot_nt(ab[0], wgu[0, cols, :])
            for q in range(1, NX):
                b = b + dot_nt(ab[q], wgu[q, cols, :])
            both = jnp.concatenate(
                [f.reshape(ny, SLOT, ct), b.reshape(ny, SLOT, ct)], axis=1
            )
            rs[:, :, cols] = both.astype(jnp.bfloat16)
            return carry

        lax.fori_loop(0, tiles, tile, 0)

    def finish(t, f_old, b_old, rr, f_out, b_out):
        sel_f = pick(routes_f[t], slots_f[t], ny, 0)
        sel_b = pick(routes_b[t], slots_b[t], ny, SLOT)

        def tile(i, total):
            cols = pl.ds(pl.multiple_of(i * ct, ct), ct)
            back = rr[:, :, cols].reshape(ny * BLK, ct)
            new = f_old[:, cols].astype(jnp.float32) + gates_f[t] * dot(sel_f, back)
            f_out[pl.ds(0, tok), cols] = new.astype(jnp.bfloat16)
            weighted = gain[:, cols] * dot(sel_b, back)
            dn[:, cols] = weighted
            xs = sv[t, :, cols].astype(jnp.float32)
            return total + jnp.sum(xs * weighted, axis=-1, keepdims=True)

        total = lax.fori_loop(0, tiles, tile, jnp.zeros((tok, 1), jnp.float32))
        r = b_scale[t]
        factor = r * r * r * (total * (1.0 / width))

        def tile2(i, carry):
            cols = pl.ds(pl.multiple_of(i * ct, ct), ct)
            xs = sv[t, :, cols].astype(jnp.float32)
            dx = b_old[:, cols].astype(jnp.float32) + (r * dn[:, cols] - xs * factor)
            b_out[pl.ds(0, tok), cols] = dx.astype(jnp.bfloat16)
            return carry

        lax.fori_loop(0, tiles, tile2, 0)

    expert_out(0, gs, r0s)
    give_back(0, r0s, r0r)
    give_wait(0, r0s, r0r, True)
    finish(0, fs, bs, r0r, xf, xb)

    sf = remote(xf, yf, ss_sem.at[0], sr_sem.at[0], (p_next, me))
    sb = remote(xb, yb, ss_sem.at[1], sr_sem.at[1], (p_prev, me))
    sf.start()
    sb.start()
    sf.wait_recv()
    sb.wait_recv()
    keep_f = jnp.where(pipe > 0, 1.0, 0.0)
    keep_b = jnp.where(pipe < npipe - 1, 1.0, 0.0)
    yf[...] = (yf[...].astype(jnp.float32) * keep_f).astype(jnp.bfloat16)
    yb[...] = (yb[...].astype(jnp.float32) * keep_b).astype(jnp.bfloat16)
    f_old = yf.at[pl.ds(0, tok)]
    b_old = yb.at[pl.ds(0, tok)]

    raw = f_old[...].astype(jnp.float32)
    nrm[...] = (raw * norm_scale(raw) * g).astype(jnp.bfloat16)
    sca[...] = (gates_b[1] * b_old[...].astype(jnp.float32)).astype(jnp.bfloat16)
    fill(
        m1,
        place(routes_f[1], slots_f[1], m_rows, 0),
        place(routes_b[1], slots_b[1], m_rows, SLOT),
    )
    scatter(2, m1, d1, 0)
    scatter_wait(2, m1, d1, 0, True)
    for q in range(NX):
        gs1[q] = dot(d1[...], wgu[q]).reshape(ny, BLK, 2 * hid)
        dh[q] = dot_nt(d1[...], wdn[pl.ds(q * hid, hid)]).reshape(ny, BLK, hid)
    expert_out(1, gs1, r1s)
    give_back(1, r1s, r1r)
    give_wait(1, r1s, r1r, True)
    finish(1, f_old, b_old, r1r, fo, bo)

    for c in w:
        c.wait_send()
    scatter_wait(0, m0, dd, 0, False)
    scatter_wait(1, mb, dd, ny * BLK, False)
    scatter_wait(2, m1, d1, 0, False)
    give_wait(0, r0s, r0r, False)
    give_wait(1, r1s, r1r, False)
    sf.wait_send()
    sb.wait_send()


def local(
    n_expert, npipe, fwd_state, bwd_state, saved_input, fwd_route, bwd_route, fwd_gate, bwd_gate,
    w_gate, w_up, w_down, norm_gain,
):
    ny = n_expert // NX
    experts = ny // PAIR
    tok, width = fwd_state.shape[1:]
    hid = w_down.shape[1]
    ct = 512
    pad = -(-tok // 16) * 16
    bf, f32 = jnp.bfloat16, jnp.float32
    vmem = pl.BlockSpec(memory_space=pltpu.VMEM)
    hbm = pl.BlockSpec(memory_space=pl.ANY)
    scratch = [
        pltpu.VMEM((NX, width, 2 * hid), bf),
        pltpu.VMEM((NX * hid, width), bf),
        pltpu.VMEM((experts * BLK, width), bf),
        pltpu.VMEM((experts * BLK, width), bf),
        pltpu.VMEM((experts * BLK, width), bf),
        pltpu.VMEM((tok, width), bf),
        pltpu.VMEM((tok, width), bf),
        pltpu.VMEM((2 * ny * BLK, width), bf),
        pltpu.VMEM((ny * BLK, width), bf),
        pltpu.VMEM((NX, 2 * ny, BLK, 2 * hid), f32),
        pltpu.VMEM((NX, ny, BLK, 2 * hid), f32),
        pltpu.VMEM((NX, ny, BLK, hid), f32),
        pltpu.VMEM((ny * SLOT, NX * hid), bf),
        pltpu.VMEM((NX, ny * SLOT, 2 * hid), bf),
        pltpu.VMEM((ny, BLK, width), bf),
        pltpu.VMEM((ny, BLK, width), bf),
        pltpu.VMEM((ny, BLK, width), bf),
        pltpu.VMEM((ny, BLK, width), bf),
        pltpu.VMEM((tok, width), f32),
        pltpu.VMEM((pad, width), bf),
        pltpu.VMEM((pad, width), bf),
        pltpu.VMEM((pad, width), bf),
        pltpu.VMEM((pad, width), bf),
        pltpu.SemaphoreType.DMA((3,)),
        pltpu.SemaphoreType.DMA((8,)),
        pltpu.SemaphoreType.DMA((8,)),
        pltpu.SemaphoreType.DMA((3, ny)),
        pltpu.SemaphoreType.DMA((3, ny)),
        pltpu.SemaphoreType.DMA((2, ny)),
        pltpu.SemaphoreType.DMA((2, ny)),
        pltpu.SemaphoreType.DMA((2,)),
        pltpu.SemaphoreType.DMA((2,)),
    ]
    fo, bo = pl.pallas_call(
        functools.partial(kernel, ny, npipe, ct),
        out_shape=[jax.ShapeDtypeStruct((tok, width), bf)] * 2,
        in_specs=[vmem] * 8 + [hbm] * 3,
        out_specs=[vmem] * 2,
        scratch_shapes=scratch,
        compiler_params=pltpu.CompilerParams(
            collective_id=0, has_side_effects=True, vmem_limit_bytes=56 << 20
        ),
    )(
        fwd_state[0], bwd_state[0], saved_input[0], fwd_route[0], bwd_route[0],
        fwd_gate[0], bwd_gate[0], norm_gain, w_gate[0], w_up[0], w_down[0],
    )
    return fo[None], bo[None]


def solution(mesh):
    placed = (
        P("pipe", "expert", None),
        P("pipe", "expert", None),
        P("pipe", None, "expert", None),
        P("pipe", None, "expert", None),
        P("pipe", None, "expert", None),
        P("pipe", None, "expert"),
        P("pipe", None, "expert"),
        P("pipe", None, "expert"),
        P("pipe", None, "expert"),
        P("pipe", "expert", None),
        P("pipe", None),
    )
    return jax.shard_map(
        functools.partial(local, mesh.shape["expert"], mesh.shape["pipe"]),
        mesh=mesh,
        in_specs=placed,
        out_specs=(P("pipe", "expert", None), P("pipe", "expert", None)),
        check_vma=False,
    )
```

time: 513 us -> 191 us (0.37)
  the two profiles are of different devices: /device:TPU:272 before, /device:TPU:257 now
where the time goes in v1:
time: 191 us
  Pallas kernels  186 us (97%)
  local copies, waits for them, and re-layouts  4.38 us (2%)
    pallas_call x1, Pallas kernels, local(): pl.pallas_call(functools.partial(kernel, ny, npipe, ct), out_shape=[jax.S...  186 us

profile of v1, /device:TPU:257, one launch (start us, length us, event | category | flops | bytes accessed | tf_op | source)
XLA Modules:
  0.0 190.8 jit_solution(8537267742667625144)
XLA Ops:
  0.6 0.0 copy-start.1
  0.6 0.7 copy-done.1
  1.3 0.0 copy-start.2
  1.3 0.7 copy.13.fr
  2.0 0.0 copy-done.2
  2.0 0.7 copy.14.br
  2.7 185.8 %shard_map.122 = (bf16[24,3584]{1,0:T(8,128)(2,1)}, bf16[24,3584]{1,0:T(8,128)(2,1)}) custom-call(bf16[24,3584]{1,0:T(8,128)(2,1)} %bitcast.18, bf16[24,3584]{1,0:T(8,128)(2,1)} %bitcast.19, bf16[2,24,3584]{2,1,0:T(8,128)(2,1)} %bitcast.15, s32[2,24,1]{2,1,0:T(8,128)} %copy.13.fr, s32[2,24,1]{2,1,0:T(8,128)} %copy.14.br, f32[2,24]{1,0:T(2,128)} %bitcast.20, ...), custom_call_target="tpu_custom_call" | custom-call | tf_op jit(solution)/shard_map/pallas_call | solution.py:392
  188.5 0.0 copy-start
  188.5 1.6 copy.17
  190.1 0.0 copy-done
  190.1 0.7 copy.18
Async XLA Ops:
  0.6 0.7 copy-start.1
  1.3 0.7 copy-start.2
  188.5 1.6 copy-start

commit v2 on v1

v2 whole, which is shorter than its diff:
```python
import functools

import jax
import jax.numpy as jnp
from jax import lax
from jax.experimental import pallas as pl
from jax.experimental.pallas import tpu as pltpu
from jax.sharding import PartitionSpec as P

EPS = 1e-06
NX = 4
PAIR = 2
SLOT = 8
BLK = 2 * SLOT
NT = (((1,), (1,)), ((), ()))


def dot(a, b):
    return jnp.dot(a, b, preferred_element_type=jnp.float32)


def dot_nt(a, b):
    return lax.dot_general(a, b, NT, preferred_element_type=jnp.float32)


def slots_of(route):
    tok = route.shape[0]
    lane = lax.broadcasted_iota(jnp.int32, (tok, 128), 1)
    hits = jnp.where(lane == route, 1.0, 0.0)
    row_i = lax.broadcasted_iota(jnp.int32, (tok, tok), 0)
    col_i = lax.broadcasted_iota(jnp.int32, (tok, tok), 1)
    lower = jnp.where(col_i < row_i, 1.0, 0.0)
    before = dot(lower.astype(jnp.bfloat16), hits.astype(jnp.bfloat16))
    return jnp.sum(before * hits, axis=1, keepdims=True).astype(jnp.int32)


def as_row(col):
    tok = col.shape[0]
    row_i = lax.broadcasted_iota(jnp.int32, (tok, tok), 0)
    col_i = lax.broadcasted_iota(jnp.int32, (tok, tok), 1)
    return jnp.sum(jnp.where(row_i == col_i, col, 0), axis=0, keepdims=True)


def as_col(row):
    tok = row.shape[1]
    row_i = lax.broadcasted_iota(jnp.int32, (tok, tok), 0)
    col_i = lax.broadcasted_iota(jnp.int32, (tok, tok), 1)
    return jnp.sum(jnp.where(row_i == col_i, row, jnp.zeros_like(row)), axis=1, keepdims=True)


def place(route, slot, rows, shift):
    target = as_row(route * BLK + (slot + shift))
    sub = lax.broadcasted_iota(jnp.int32, (rows, route.shape[0]), 0)
    return jnp.where(sub == target, 1.0, 0.0).astype(jnp.bfloat16)


def pick(route, slot, expert_of, shift):
    lane = lax.broadcasted_iota(jnp.int32, (route.shape[0], expert_of.shape[1]), 1)
    mine = (lane % BLK == slot + shift) & (expert_of == route)
    return jnp.where(mine, 1.0, 0.0).astype(jnp.bfloat16)


def kernel(
    ny, npipe, ct,
    fs, bs, sv, fr, br, fg, bg, gain, wg, wu, wd,
    fo, bo,
    wgu, wdn, m0, mb, m1, nrm, sca, dd, d1, gs, gs1, dh, hs, ab, po,
    xs0, xr0, rs0, rr0, xs1, xr1, rs1, rr1, dn, xf, xb, yf, yb,
    l_sem, ws_sem, wr_sem, ds_sem, dr_sem, es_sem, er_sem, cs_sem, cr_sem, rs_sem, rr_sem, ss_sem, sr_sem,
):
    width = wd.shape[1]
    hid = wd.shape[0]
    tok = fs.shape[0]
    tiles = width // ct
    ns = ny // PAIR
    me = lax.axis_index("expert")
    pipe = lax.axis_index("pipe")
    y, x = me // NX, me % NX
    sg = 1 - 2 * (y % 2)
    core = pipe % 2
    p_next = (pipe + 1) % npipe
    p_prev = (pipe + npipe - 1) % npipe
    mesh_id = pl.DeviceIdType.MESH

    def at_row(row):
        return (pipe, ((row + ny) % ny) * NX + x)

    def at_col(col):
        return (pipe, y * NX + (col + NX) % NX)

    def source_row(j):
        return (y - sg * j + ny) % ny

    def target_row(j):
        return (y + (sg * j if j % 2 == 0 else -sg * j) + ny) % ny

    partner = at_row(y + sg)
    across = at_col(x + 2)
    taker = at_col(x + 3 + 2 * core)

    loads = [
        pltpu.make_async_copy(wg, wgu.at[0, :, pl.ds(0, hid)], l_sem.at[0]),
        pltpu.make_async_copy(wu, wgu.at[0, :, pl.ds(hid, hid)], l_sem.at[1]),
        pltpu.make_async_copy(wd, wdn.at[pl.ds(0, hid)], l_sem.at[2]),
    ]
    for c in loads:
        c.start()

    barrier = pltpu.get_barrier_semaphore()
    peers = [at_row(y + k) for k in range(1, ny)] + [at_col(x + k) for k in range(1, NX)]
    peers += [(p_next, me), (p_prev, me)]
    for dev in peers:
        pl.semaphore_signal(barrier, inc=1, device_id=dev, device_id_type=mesh_id)

    def remote(src, dst, send, recv, dev):
        return pltpu.make_async_remote_copy(
            src_ref=src, dst_ref=dst, send_sem=send, recv_sem=recv,
            device_id=dev, device_id_type=mesh_id,
        )

    def part(q, i):
        if i < 4:
            return wgu.at[q, pl.ds(i * (width // 4), width // 4)]
        return wdn.at[pl.ds(q * hid + (i - 4) * (hid // 2), hid // 2)]

    to_partner = [remote(part(0, i), part(2, i), ws_sem.at[i], wr_sem.at[i], partner) for i in range(6)]
    to_taker = [
        remote(wgu.at[0], wgu.at[1], ws_sem.at[6], wr_sem.at[6], taker),
        remote(wdn.at[pl.ds(0, hid)], wdn.at[pl.ds(hid, hid)], ws_sem.at[7], wr_sem.at[7], taker),
    ]
    passed = [remote(part(2, i), part(3, i), ws_sem.at[8 + i], wr_sem.at[8 + i], taker) for i in range(6)]
    far_first = list(range(ns - 1, 0, -1))

    def blk(ref, i):
        start = i * BLK if isinstance(i, int) else pl.multiple_of(i * BLK, BLK)
        return ref.at[pl.ds(start, BLK)]

    def send_copy(phase, m, d, base, j):
        return remote(
            blk(m, target_row(j) // PAIR), blk(d, base + j),
            ds_sem.at[phase, j], dr_sem.at[phase, j], at_row(target_row(j)),
        )

    def pass_copy(phase, d, base, j):
        return remote(
            blk(d, base + j), blk(d, base + ns + j), es_sem.at[phase, j], er_sem.at[phase, j], across
        )

    def scatter(phase, m, d, base):
        for j in far_first:
            send_copy(phase, m, d, base, j).start()
        blk(d, base)[...] = blk(m, y // PAIR)[...]
        pass_copy(phase, d, base, 0).start()

    def scatter_pass(phase, m, d, base):
        for j in range(1, ns):
            send_copy(phase, m, d, base, j).wait_recv()
            pass_copy(phase, d, base, j).start()

    def scatter_end(phase, d, base):
        for j in range(ns):
            pass_copy(phase, d, base, j).wait_recv()

    def norm_scale(raw):
        return lax.rsqrt(jnp.mean(raw * raw, axis=-1, keepdims=True) + EPS)

    g = gain[...]
    routes_f = [as_col(fr[pl.ds(t, 1), :]) for t in range(2)]
    routes_b = [as_col(br[pl.ds(t, 1), :]) for t in range(2)]
    slots_f = [slots_of(r) for r in routes_f]
    slots_b = [slots_of(r) for r in routes_b]
    gates_f = [as_col(fg[pl.ds(t, 1), :]) for t in range(2)]
    gates_b = [as_col(bg[pl.ds(t, 1), :]) for t in range(2)]
    m_rows = m0.shape[0]

    def fill(m, pa, pb):
        def tile(i, carry):
            cols = pl.ds(pl.multiple_of(i * ct, ct), ct)
            m[:, cols] = (dot(pa, nrm[:, cols]) + dot(pb, sca[:, cols])).astype(jnp.bfloat16)
            return carry

        lax.fori_loop(0, tiles, tile, 0)

    raw = fs[...].astype(jnp.float32)
    nrm[...] = (raw * norm_scale(raw) * g).astype(jnp.bfloat16)
    sca[...] = (gates_b[0] * bs[...].astype(jnp.float32)).astype(jnp.bfloat16)
    fill(
        m0,
        place(routes_f[0], slots_f[0], m_rows, 0),
        place(routes_b[0], slots_b[0], m_rows, SLOT),
    )
    pl.semaphore_wait(barrier, len(peers))
    scatter(0, m0, dd, 0)
    loads[0].wait()
    loads[1].wait()
    to_partner[0].start()
    to_taker[0].start()
    b_scale = []
    for t, dst in ((0, nrm), (1, sca)):
        raw = sv[t].astype(jnp.float32)
        scale = norm_scale(raw)
        b_scale.append(scale)
        dst[...] = (raw * scale * g).astype(jnp.bfloat16)
    fill(
        mb,
        place(routes_b[0], slots_b[0], m_rows, 0),
        place(routes_b[1], slots_b[1], m_rows, SLOT),
    )
    scatter(1, mb, dd, ny)
    loads[2].wait()
    for c in to_partner[1:]:
        c.start()
    scatter_pass(0, m0, dd, 0)
    scatter_pass(1, mb, dd, ny)
    to_taker[1].start()

    def into_hidden(q):
        gs[q] = dot(dd[...], wgu[q]).reshape(2 * ny, BLK, 2 * hid)
        dh[q] = dot_nt(dd[pl.ds(0, ny * BLK)], wdn[pl.ds(q * hid, hid)]).reshape(ny, BLK, hid)

    for i in range(2):
        to_partner[i].wait_recv()
        passed[i].start()
    scatter_end(0, dd, 0)
    scatter_end(1, dd, ny)
    into_hidden(0)
    for i in range(2, 4):
        to_partner[i].wait_recv()
        passed[i].start()
    for c in to_taker:
        c.wait_recv()
    into_hidden(1)
    for i in range(4, 6):
        to_partner[i].wait_recv()
        passed[i].start()
    into_hidden(2)
    for c in passed:
        c.wait_recv()
    into_hidden(3)

    rows = ny * SLOT

    def expert_out(t, gf, xs):
        for q in range(NX):
            f = gf[q, pl.ds(0, ny), pl.ds(0, SLOT), :].reshape(rows, 2 * hid)
            gated, upped = f[:, :hid], f[:, hid:]
            hidden = gated * jax.nn.sigmoid(gated) * upped
            hs[:, pl.ds(q * hid, hid)] = hidden.astype(jnp.bfloat16)
            b = gs[q, pl.ds(ny, ny), pl.ds(t * SLOT, SLOT), :].reshape(rows, 2 * hid)
            gated, upped = b[:, :hid], b[:, hid:]
            dhid = dh[q, :, pl.ds(SLOT, SLOT), :].reshape(rows, hid)
            s = jax.nn.sigmoid(gated)
            da = dhid * upped * s * (1.0 + gated * (1.0 - s))
            db = dhid * gated * s
            ab[q, :, pl.ds(0, hid)] = da.astype(jnp.bfloat16)
            ab[q, :, pl.ds(hid, hid)] = db.astype(jnp.bfloat16)

        def tile(i, carry):
            cols = pl.ds(pl.multiple_of(i * ct, ct), ct)
            f = dot(hs[...], wdn[:, cols])
            b = dot_nt(ab[0], wgu[0, cols, :])
            for q in range(1, NX):
                b = b + dot_nt(ab[q], wgu[q, cols, :])
            both = jnp.concatenate(
                [f.reshape(ny, SLOT, ct), b.reshape(ny, SLOT, ct)], axis=1
            )
            po[:, :, cols] = both[:ns]
            xs[:, :, cols] = both[ns:].astype(jnp.bfloat16)
            return carry

        lax.fori_loop(0, tiles, tile, 0)

    def half_copy(t, xs, xr, j):
        return remote(xs.at[j], xr.at[j], cs_sem.at[t, j], cr_sem.at[t, j], across)

    def back_copy(t, rs, rr, j):
        return remote(rs.at[j], rr.at[j], rs_sem.at[t, j], rr_sem.at[t, j], at_row(source_row(j)))

    def give_back(t, xs, xr, rs, rr):
        for j in far_first + [0]:
            half_copy(t, xs, xr, j).start()
        for j in far_first + [0]:
            half_copy(t, xs, xr, j).wait_recv()
            (rs if j else rr)[j] = (po[j] + xr[j].astype(jnp.float32)).astype(jnp.bfloat16)
            if j:
                back_copy(t, rs, rr, j).start()
        for j in range(1, ns):
            remote(
                rs.at[j], rr.at[j], rs_sem.at[t, j], rr_sem.at[t, j], at_row(target_row(j))
            ).wait_recv()

    jb = lax.broadcasted_iota(jnp.int32, (tok, ns * BLK), 1) // BLK
    step = jnp.where(jb % 2 == 0, jb, -jb) * sg
    expert_of = ((y + step + ny) % ny) // PAIR

    def finish(t, f_old, b_old, rr, f_out, b_out, after_f=None):
        sel_f = pick(routes_f[t], slots_f[t], expert_of, 0)
        sel_b = pick(routes_b[t], slots_b[t], expert_of, SLOT)

        def tile(i, total):
            cols = pl.ds(pl.multiple_of(i * ct, ct), ct)
            back = rr[:, :, cols].reshape(ns * BLK, ct)
            new = f_old[:, cols].astype(jnp.float32) + gates_f[t] * dot(sel_f, back)
            f_out[pl.ds(0, tok), cols] = new.astype(jnp.bfloat16)
            weighted = gain[:, cols] * dot(sel_b, back)
            dn[:, cols] = weighted
            xs = sv[t, :, cols].astype(jnp.float32)
            return total + jnp.sum(xs * weighted, axis=-1, keepdims=True)

        total = lax.fori_loop(0, tiles, tile, jnp.zeros((tok, 1), jnp.float32))
        if after_f is not None:
            after_f()
        r = b_scale[t]
        factor = r * r * r * (total * (1.0 / width))

        def tile2(i, carry):
            cols = pl.ds(pl.multiple_of(i * ct, ct), ct)
            xs = sv[t, :, cols].astype(jnp.float32)
            dx = b_old[:, cols].astype(jnp.float32) + (r * dn[:, cols] - xs * factor)
            b_out[pl.ds(0, tok), cols] = dx.astype(jnp.bfloat16)
            return carry

        lax.fori_loop(0, tiles, tile2, 0)

    expert_out(0, gs, xs0)
    give_back(0, xs0, xr0, rs0, rr0)

    sf = remote(xf, yf, ss_sem.at[0], sr_sem.at[0], (p_next, me))
    sb = remote(xb, yb, ss_sem.at[1], sr_sem.at[1], (p_prev, me))
    finish(0, fs, bs, rr0, xf, xb, sf.start)
    sb.start()
    sf.wait_recv()
    keep_f = jnp.where(pipe > 0, 1.0, 0.0)
    keep_b = jnp.where(pipe < npipe - 1, 1.0, 0.0)
    yf[...] = (yf[...].astype(jnp.float32) * keep_f).astype(jnp.bfloat16)
    f_old = yf.at[pl.ds(0, tok)]
    b_old = yb.at[pl.ds(0, tok)]

    raw = f_old[...].astype(jnp.float32)
    nrm[...] = (raw * norm_scale(raw) * g).astype(jnp.bfloat16)
    sb.wait_recv()
    yb[...] = (yb[...].astype(jnp.float32) * keep_b).astype(jnp.bfloat16)
    sca[...] = (gates_b[1] * b_old[...].astype(jnp.float32)).astype(jnp.bfloat16)
    fill(
        m1,
        place(routes_f[1], slots_f[1], m_rows, 0),
        place(routes_b[1], slots_b[1], m_rows, SLOT),
    )
    scatter(2, m1, d1, 0)
    scatter_pass(2, m1, d1, 0)
    scatter_end(2, d1, 0)
    for q in range(NX):
        gs1[q] = dot(d1[...], wgu[q]).reshape(ny, BLK, 2 * hid)
        dh[q] = dot_nt(d1[...], wdn[pl.ds(q * hid, hid)]).reshape(ny, BLK, hid)
    expert_out(1, gs1, xs1)
    give_back(1, xs1, xr1, rs1, rr1)
    finish(1, f_old, b_old, rr1, fo, bo)

    for c in to_partner + to_taker + passed:
        c.wait_send()
    for phase, m, d, base in ((0, m0, dd, 0), (1, mb, dd, ny), (2, m1, d1, 0)):
        for j in range(ns):
            if j:
                send_copy(phase, m, d, base, j).wait_send()
            pass_copy(phase, d, base, j).wait_send()
    for t, xs, xr, rs, rr in ((0, xs0, xr0, rs0, rr0), (1, xs1, xr1, rs1, rr1)):
        for j in range(ns):
            half_copy(t, xs, xr, j).wait_send()
            if j:
                back_copy(t, rs, rr, j).wait_send()
    sf.wait_send()
    sb.wait_send()


def local(
    n_expert, npipe, fwd_state, bwd_state, saved_input, fwd_route, bwd_route, fwd_gate, bwd_gate,
    w_gate, w_up, w_down, norm_gain,
):
    ny = n_expert // NX
    experts = ny // PAIR
    tok, width = fwd_state.shape[1:]
    hid = w_down.shape[1]
    ct = 512
    pad = -(-tok // 16) * 16
    bf, f32 = jnp.bfloat16, jnp.float32
    vmem = pl.BlockSpec(memory_space=pltpu.VMEM)
    hbm = pl.BlockSpec(memory_space=pl.ANY)
    ns = ny // PAIR
    scratch = [
        pltpu.VMEM((NX, width, 2 * hid), bf),
        pltpu.VMEM((NX * hid, width), bf),
        pltpu.VMEM((experts * BLK, width), bf),
        pltpu.VMEM((experts * BLK, width), bf),
        pltpu.VMEM((experts * BLK, width), bf),
        pltpu.VMEM((tok, width), bf),
        pltpu.VMEM((tok, width), bf),
        pltpu.VMEM((2 * ny * BLK, width), bf),
        pltpu.VMEM((ny * BLK, width), bf),
        pltpu.VMEM((NX, 2 * ny, BLK, 2 * hid), f32),
        pltpu.VMEM((NX, ny, BLK, 2 * hid), f32),
        pltpu.VMEM((NX, ny, BLK, hid), f32),
        pltpu.VMEM((ny * SLOT, NX * hid), bf),
        pltpu.VMEM((NX, ny * SLOT, 2 * hid), bf),
        pltpu.VMEM((ns, BLK, width), f32),
    ]
    scratch += [pltpu.VMEM((ns, BLK, width), bf)] * 8
    scratch += [
        pltpu.VMEM((tok, width), f32),
        pltpu.VMEM((pad, width), bf),
        pltpu.VMEM((pad, width), bf),
        pltpu.VMEM((pad, width), bf),
        pltpu.VMEM((pad, width), bf),
    ]
    scratch += [
        pltpu.SemaphoreType.DMA(shape)
        for shape in (
            (3,), (14,), (14,), (3, ns), (3, ns), (3, ns), (3, ns), (2, ns), (2, ns), (2, ns), (2, ns),
            (2,), (2,),
        )
    ]
    fo, bo = pl.pallas_call(
        functools.partial(kernel, ny, npipe, ct),
        out_shape=[jax.ShapeDtypeStruct((tok, width), bf)] * 2,
        in_specs=[vmem] * 8 + [hbm] * 3,
        out_specs=[vmem] * 2,
        scratch_shapes=scratch,
        compiler_params=pltpu.CompilerParams(
            collective_id=0, has_side_effects=True, vmem_limit_bytes=56 << 20
        ),
    )(
        fwd_state[0], bwd_state[0], saved_input[0], fwd_route.reshape(2, tok), bwd_route.reshape(2, tok),
        fwd_gate[0], bwd_gate[0], norm_gain, w_gate[0], w_up[0], w_down[0],
    )
    return fo[None], bo[None]


def solution(mesh):
    placed = (
        P("pipe", "expert", None),
        P("pipe", "expert", None),
        P("pipe", None, "expert", None),
        P("pipe", None, "expert", None),
        P("pipe", None, "expert", None),
        P("pipe", None, "expert"),
        P("pipe", None, "expert"),
        P("pipe", None, "expert"),
        P("pipe", None, "expert"),
        P("pipe", "expert", None),
        P("pipe", None),
    )
    return jax.shard_map(
        functools.partial(local, mesh.shape["expert"], mesh.shape["pipe"]),
        mesh=mesh,
        in_specs=placed,
        out_specs=(P("pipe", "expert", None), P("pipe", "expert", None)),
        check_vma=False,
    )
```

time: 191 us -> 168 us (0.88)
  the two profiles are of different devices: /device:TPU:257 before, /device:TPU:388 now
where the time goes in v2:
time: 168 us
  Pallas kernels  165 us (98%)
  local copies, waits for them, and re-layouts  2.31 us (1%)
    pallas_call x1, Pallas kernels, local(): pl.pallas_call(functools.partial(kernel, ny, npipe, ct), out_shape=[jax.S...  165 us

profile of v2, /device:TPU:388, one launch (start us, length us, event | category | flops | bytes accessed | tf_op | source)
XLA Modules:
  0.0 167.7 jit_solution(7244117535400609419)
XLA Ops:
  0.6 164.7 %shard_map.122 = (bf16[24,3584]{1,0:T(8,128)(2,1)}, bf16[24,3584]{1,0:T(8,128)(2,1)}) custom-call(bf16[24,3584]{1,0:T(8,128)(2,1)} %bitcast.18, bf16[24,3584]{1,0:T(8,128)(2,1)} %bitcast.19, bf16[2,24,3584]{2,1,0:T(8,128)(2,1)} %bitcast.15, s32[2,24]{1,0:T(2,128)} %bitcast.20, s32[2,24]{1,0:T(2,128)} %bitcast.21, f32[2,24]{1,0:T(2,128)} %bitcast.22, ...), custom_call_target="tpu_custom_call" | custom-call | tf_op jit(solution)/shard_map/pallas_call | solution.py:421
  165.4 0.0 copy-start
  165.4 1.6 copy.15
  167.0 0.0 copy-done
  167.0 0.7 copy.16
Async XLA Ops:
  165.4 1.6 copy-start

commit v3 on v2

v3 whole, which is shorter than its diff:
```python
import functools

import jax
import jax.numpy as jnp
from jax import lax
from jax.experimental import pallas as pl
from jax.experimental.pallas import tpu as pltpu
from jax.sharding import PartitionSpec as P

EPS = 1e-06
NX = 4
PAIR = 2
SLOT = 8
BLK = 2 * SLOT
NT = (((1,), (1,)), ((), ()))


def dot(a, b):
    return jnp.dot(a, b, preferred_element_type=jnp.float32)


def dot_nt(a, b):
    return lax.dot_general(a, b, NT, preferred_element_type=jnp.float32)


def slots_of(route):
    tok = route.shape[0]
    lane = lax.broadcasted_iota(jnp.int32, (tok, 128), 1)
    hits = jnp.where(lane == route, 1.0, 0.0)
    row_i = lax.broadcasted_iota(jnp.int32, (tok, tok), 0)
    col_i = lax.broadcasted_iota(jnp.int32, (tok, tok), 1)
    lower = jnp.where(col_i < row_i, 1.0, 0.0)
    before = dot(lower.astype(jnp.bfloat16), hits.astype(jnp.bfloat16))
    return jnp.sum(before * hits, axis=1, keepdims=True).astype(jnp.int32)


def as_row(col):
    tok = col.shape[0]
    row_i = lax.broadcasted_iota(jnp.int32, (tok, tok), 0)
    col_i = lax.broadcasted_iota(jnp.int32, (tok, tok), 1)
    return jnp.sum(jnp.where(row_i == col_i, col, 0), axis=0, keepdims=True)


def as_col(row):
    tok = row.shape[1]
    row_i = lax.broadcasted_iota(jnp.int32, (tok, tok), 0)
    col_i = lax.broadcasted_iota(jnp.int32, (tok, tok), 1)
    return jnp.sum(jnp.where(row_i == col_i, row, jnp.zeros_like(row)), axis=1, keepdims=True)


def place(route, slot, rows, shift):
    target = as_row(route * BLK + (slot + shift))
    sub = lax.broadcasted_iota(jnp.int32, (rows, route.shape[0]), 0)
    return jnp.where(sub == target, 1.0, 0.0).astype(jnp.bfloat16)


def pick(route, slot, expert_of, shift):
    lane = lax.broadcasted_iota(jnp.int32, (route.shape[0], expert_of.shape[1]), 1)
    mine = (lane % BLK == slot + shift) & (expert_of == route)
    return jnp.where(mine, 1.0, 0.0).astype(jnp.bfloat16)


def kernel(
    ny, npipe, ct,
    fs, bs, sv, fr, br, fg, bg, gain, wg, wu, wd,
    fo, bo,
    wgu, wdn, mm, rows_in, dd, gs, dh, hs, ab, po, xs, xr, rs, rr, dn, xf, xb, yf, yb,
    l_sem, ws_sem, wr_sem, ds_sem, dr_sem, es_sem, er_sem, cs_sem, cr_sem, rs_sem, rr_sem, ss_sem, sr_sem,
):
    width = wd.shape[1]
    hid = wd.shape[0]
    tok = fs.shape[0]
    half = width // 2
    tiles = half // ct
    groups = ny // PAIR
    ns = ny // PAIR
    me = lax.axis_index("expert")
    pipe = lax.axis_index("pipe")
    y, x = me // NX, me % NX
    sg = 1 - 2 * (y % 2)
    core = pipe % 2
    p_next = (pipe + 1) % npipe
    p_prev = (pipe + npipe - 1) % npipe
    mesh_id = pl.DeviceIdType.MESH

    def at_row(row):
        return (pipe, ((row + ny) % ny) * NX + x)

    def at_col(col):
        return (pipe, y * NX + (col + NX) % NX)

    def source_row(j):
        return (y - sg * j + ny) % ny

    def target_row(j):
        return (y + (sg * j if j % 2 == 0 else -sg * j) + ny) % ny

    partner = at_row(y + sg)
    across = at_col(x + 2)
    taker = at_col(x + 3 + 2 * core)

    loads = [
        pltpu.make_async_copy(wg, wgu.at[0, :, pl.ds(0, hid)], l_sem.at[0]),
        pltpu.make_async_copy(wu, wgu.at[0, :, pl.ds(hid, hid)], l_sem.at[1]),
        pltpu.make_async_copy(wd, wdn.at[pl.ds(0, hid)], l_sem.at[2]),
    ]
    for c in loads:
        c.start()

    barrier = pltpu.get_barrier_semaphore()
    peers = [at_row(y + k) for k in range(1, ny)] + [at_col(x + k) for k in range(1, NX)]
    peers += [(p_next, me), (p_prev, me)]
    for dev in peers:
        pl.semaphore_signal(barrier, inc=1, device_id=dev, device_id_type=mesh_id)

    def remote(src, dst, send, recv, dev):
        return pltpu.make_async_remote_copy(
            src_ref=src, dst_ref=dst, send_sem=send, recv_sem=recv,
            device_id=dev, device_id_type=mesh_id,
        )

    def part(q, i):
        if i < 4:
            return wgu.at[q, pl.ds(i * (width // 4), width // 4)]
        return wdn.at[pl.ds(q * hid + (i - 4) * (hid // 4), hid // 4)]

    to_partner = [remote(part(0, i), part(2, i), ws_sem.at[i], wr_sem.at[i], partner) for i in range(8)]
    to_taker = [
        remote(wgu.at[0], wgu.at[1], ws_sem.at[16], wr_sem.at[16], taker),
        remote(wdn.at[pl.ds(0, hid)], wdn.at[pl.ds(hid, hid)], ws_sem.at[17], wr_sem.at[17], taker),
    ]
    passed = [remote(part(2, i), part(3, i), ws_sem.at[8 + i], wr_sem.at[8 + i], taker) for i in range(8)]
    far_first = list(range(ns - 1, 0, -1))

    def blk(ref, i):
        start = i * BLK if isinstance(i, int) else pl.multiple_of(i * BLK, BLK)
        return ref.at[pl.ds(start, BLK)]

    def send_copy(kind, j):
        return remote(
            blk(mm, kind * groups + target_row(j) // PAIR), blk(dd, kind * ny + j),
            ds_sem.at[kind, j], dr_sem.at[kind, j], at_row(target_row(j)),
        )

    def pass_copy(kind, j):
        return remote(
            blk(dd, kind * ny + j), blk(dd, kind * ny + ns + j),
            es_sem.at[kind, j], er_sem.at[kind, j], across,
        )

    def scatter(kind):
        for j in far_first:
            send_copy(kind, j).start()
        blk(dd, kind * ny)[...] = blk(mm, kind * groups + y // PAIR)[...]
        pass_copy(kind, 0).start()

    def scatter_pass(kind):
        for j in range(1, ns):
            send_copy(kind, j).wait_recv()
            pass_copy(kind, j).start()

    def scatter_end(kind):
        for j in range(ns):
            pass_copy(kind, j).wait_recv()

    def norm_scale(raw):
        return lax.rsqrt(jnp.mean(raw * raw, axis=-1, keepdims=True) + EPS)

    g = gain[...]
    routes_f = [as_col(fr[pl.ds(t, 1), :]) for t in range(2)]
    routes_b = [as_col(br[pl.ds(t, 1), :]) for t in range(2)]
    slots_f = [slots_of(r) for r in routes_f]
    slots_b = [slots_of(r) for r in routes_b]
    gates_f = [as_col(fg[pl.ds(t, 1), :]) for t in range(2)]
    gates_b = [as_col(bg[pl.ds(t, 1), :]) for t in range(2)]

    def fill(kind, route, slot, values):
        rows_in[...] = values.astype(jnp.bfloat16)
        lo = place(route, slot, groups * BLK, 0)
        hi = place(route, slot, groups * BLK, SLOT)

        def tile(i, carry):
            start = pl.multiple_of(i * ct, ct)
            cols = pl.ds(start, ct)
            cols2 = pl.ds(pl.multiple_of(half + start, 128), ct)
            both = dot(lo, rows_in[:, cols]) + dot(hi, rows_in[:, cols2])
            mm[pl.ds(kind * groups * BLK, groups * BLK), cols] = both.astype(jnp.bfloat16)
            return carry

        lax.fori_loop(0, tiles, tile, 0)

    def fill_tokens(kind, t, state):
        raw = state[...].astype(jnp.float32)
        fill(kind, routes_f[t], slots_f[t], raw * norm_scale(raw) * g)

    def fill_grads(kind, t, state):
        fill(kind, routes_b[t], slots_b[t], gates_b[t] * state[...].astype(jnp.float32))

    def fill_saved(kind, t):
        raw = sv[t].astype(jnp.float32)
        scale = norm_scale(raw)
        fill(kind, routes_b[t], slots_b[t], raw * scale * g)
        return scale

    fill_tokens(0, 0, fs)
    pl.semaphore_wait(barrier, len(peers))
    scatter(0)
    loads[0].wait()
    loads[1].wait()
    to_partner[0].start()
    to_taker[0].start()
    fill_grads(2, 0, bs)
    scatter(2)
    b_scale = [fill_saved(1, 0)]
    scatter(1)
    loads[2].wait()
    for c in to_partner[1:]:
        c.start()
    b_scale.append(fill_saved(3, 1))
    for kind in (0, 2, 1):
        scatter_pass(kind)
    to_taker[1].start()
    for j in far_first:
        send_copy(3, j).start()
    blk(dd, 3 * ny)[...] = blk(mm, 3 * groups + y // PAIR)[...]

    def folded(kind, count, product, w_lo, w_hi):
        a = dd[pl.ds(kind * ny * BLK, count * ny * BLK)]
        lo = product(a, w_lo).reshape(count * ny, BLK, -1)[:, :SLOT]
        hi = product(a, w_hi).reshape(count * ny, BLK, -1)[:, SLOT:]
        return lo + hi

    def through_up(q, kind, count, at):
        gs[q, pl.ds(at * ny, count * ny)] = folded(
            kind, count, dot, wgu[q, pl.ds(0, half)], wgu[q, pl.ds(half, half)]
        )

    def through_down(q, kind, t):
        w_q = wdn.at[pl.ds(q * hid, hid)]
        dh[q, pl.ds(t * ny, ny)] = folded(
            kind, 1, dot_nt, w_q[:, pl.ds(0, half)], w_q[:, pl.ds(half, half)]
        )

    def into_hidden(q):
        through_up(q, 0, 2, 0)
        through_down(q, 2, 0)

    for i in range(2):
        to_partner[i].wait_recv()
        passed[i].start()
    for kind in (0, 2, 1):
        scatter_end(kind)
    into_hidden(0)
    for i in range(2, 4):
        to_partner[i].wait_recv()
        passed[i].start()
    for c in to_taker:
        c.wait_recv()
    into_hidden(1)
    for i in range(4, 8):
        to_partner[i].wait_recv()
        passed[i].start()
    into_hidden(2)
    for c in passed:
        c.wait_recv()
    into_hidden(3)

    rows = ny * SLOT

    def put_out(c, i, lo, hi):
        cols = pl.ds(pl.multiple_of(i * ct, ct), ct)
        both = jnp.concatenate([lo.reshape(ny, SLOT, ct), hi.reshape(ny, SLOT, ct)], axis=1)
        po[c % 2, :, :, cols] = both[:ns]
        xs[c, :, :, cols] = both[ns:].astype(jnp.bfloat16)

    def out_f(t, at):
        for q in range(NX):
            f = gs[q, pl.ds(at * ny, ny)].reshape(rows, 2 * hid)
            gated, upped = f[:, :hid], f[:, hid:]
            hidden = gated * jax.nn.sigmoid(gated) * upped
            hs[:, pl.ds(q * hid, hid)] = hidden.astype(jnp.bfloat16)

        def tile(i, carry):
            start = pl.multiple_of(i * ct, ct)
            lo = dot(hs[...], wdn[:, pl.ds(start, ct)])
            hi = dot(hs[...], wdn[:, pl.ds(pl.multiple_of(half + start, 128), ct)])
            put_out(2 * t, i, lo, hi)
            return carry

        lax.fori_loop(0, tiles, tile, 0)
        half_start(2 * t)

    def out_b(t, at):
        for q in range(NX):
            b = gs[q, pl.ds(at * ny, ny)].reshape(rows, 2 * hid)
            gated, upped = b[:, :hid], b[:, hid:]
            dhid = dh[q, pl.ds(t * ny, ny)].reshape(rows, hid)
            s = jax.nn.sigmoid(gated)
            da = dhid * upped * s * (1.0 + gated * (1.0 - s))
            db = dhid * gated * s
            ab[q, :, pl.ds(0, hid)] = da.astype(jnp.bfloat16)
            ab[q, :, pl.ds(hid, hid)] = db.astype(jnp.bfloat16)

        def through(start):
            b = dot_nt(ab[0], wgu[0, pl.ds(start, ct), :])
            for q in range(1, NX):
                b = b + dot_nt(ab[q], wgu[q, pl.ds(start, ct), :])
            return b

        def tile(i, carry):
            start = pl.multiple_of(i * ct, ct)
            put_out(2 * t + 1, i, through(start), through(pl.multiple_of(half + start, 128)))
            return carry

        lax.fori_loop(0, tiles, tile, 0)
        half_start(2 * t + 1)

    def half_copy(c, j):
        return remote(xs.at[c, j], xr.at[c, j], cs_sem.at[c, j], cr_sem.at[c, j], across)

    def back_copy(c, j):
        return remote(rs.at[c, j], rr.at[c, j], rs_sem.at[c, j], rr_sem.at[c, j], at_row(source_row(j)))

    def half_start(c):
        for j in far_first + [0]:
            half_copy(c, j).start()

    def back_start(c):
        for j in far_first + [0]:
            half_copy(c, j).wait_recv()
            (rs if j else rr)[c, j] = (po[c % 2, j] + xr[c, j].astype(jnp.float32)).astype(jnp.bfloat16)
            if j:
                back_copy(c, j).start()

    def back_wait(c):
        for j in range(1, ns):
            back_copy(c, j).wait_recv()

    jb = lax.broadcasted_iota(jnp.int32, (tok, ns * BLK), 1) // BLK
    step = jnp.where(jb % 2 == 0, jb, -jb) * sg
    expert_of = ((y + step + ny) % ny) // PAIR

    def both_halves(i):
        start = pl.multiple_of(i * ct, ct)
        return pl.ds(start, ct), (pl.ds(start, ct), pl.ds(pl.multiple_of(half + start, 128), ct))

    def finish_f(t, old, out):
        sel = [pick(routes_f[t], slots_f[t], expert_of, shift) for shift in (0, SLOT)]

        def tile(i, carry):
            cols, wide = both_halves(i)
            back = rr[2 * t, :, :, cols].reshape(ns * BLK, ct)
            for s, w in zip(sel, wide):
                new = old[:, w].astype(jnp.float32) + gates_f[t] * dot(s, back)
                out[pl.ds(0, tok), w] = new.astype(jnp.bfloat16)
            return carry

        lax.fori_loop(0, tiles, tile, 0)

    def finish_b(t, old, out):
        sel = [pick(routes_b[t], slots_b[t], expert_of, shift) for shift in (0, SLOT)]

        def tile(i, total):
            cols, wide = both_halves(i)
            back = rr[2 * t + 1, :, :, cols].reshape(ns * BLK, ct)
            for s, w in zip(sel, wide):
                weighted = gain[:, w] * dot(s, back)
                dn[:, w] = weighted
                total = total + jnp.sum(
                    sv[t, :, w].astype(jnp.float32) * weighted, axis=-1, keepdims=True
                )
            return total

        total = lax.fori_loop(0, tiles, tile, jnp.zeros((tok, 1), jnp.float32))
        r = b_scale[t]
        factor = r * r * r * (total * (1.0 / width))

        def tile2(i, carry):
            for w in both_halves(i)[1]:
                saved = sv[t, :, w].astype(jnp.float32)
                dx = old[:, w].astype(jnp.float32) + (r * dn[:, w] - saved * factor)
                out[pl.ds(0, tok), w] = dx.astype(jnp.bfloat16)
            return carry

        lax.fori_loop(0, tiles, tile2, 0)

    out_f(0, 0)
    out_b(0, 1)
    back_start(0)
    back_start(1)
    pass_copy(3, 0).start()
    scatter_pass(3)

    sf = remote(xf, yf, ss_sem.at[0], sr_sem.at[0], (p_next, me))
    sb = remote(xb, yb, ss_sem.at[1], sr_sem.at[1], (p_prev, me))
    back_wait(0)
    finish_f(0, fs, xf)
    sf.start()
    back_wait(1)
    finish_b(0, bs, xb)
    sb.start()
    scatter_end(3)
    for q in range(NX):
        through_up(q, 3, 1, 2)
    keep_f = jnp.where(pipe > 0, 1.0, 0.0)
    keep_b = jnp.where(pipe < npipe - 1, 1.0, 0.0)
    f_old = yf.at[pl.ds(0, tok)]
    b_old = yb.at[pl.ds(0, tok)]

    sf.wait_recv()
    yf[...] = (yf[...].astype(jnp.float32) * keep_f).astype(jnp.bfloat16)
    fill_tokens(4, 1, f_old)
    scatter(4)
    sb.wait_recv()
    yb[...] = (yb[...].astype(jnp.float32) * keep_b).astype(jnp.bfloat16)
    fill_grads(5, 1, b_old)
    scatter(5)
    scatter_pass(4)
    scatter_pass(5)
    scatter_end(4)
    for q in range(NX):
        through_up(q, 4, 1, 3)
    out_f(1, 3)
    scatter_end(5)
    for q in range(NX):
        through_down(q, 5, 1)
    out_b(1, 2)
    back_start(2)
    back_start(3)
    back_wait(2)
    finish_f(1, f_old, fo)
    back_wait(3)
    finish_b(1, b_old, bo)

    for c in to_partner + to_taker + passed:
        c.wait_send()
    for kind in range(6):
        for j in range(ns):
            if j:
                send_copy(kind, j).wait_send()
            pass_copy(kind, j).wait_send()
    for c in range(4):
        for j in range(ns):
            half_copy(c, j).wait_send()
            if j:
                back_copy(c, j).wait_send()
    sf.wait_send()
    sb.wait_send()


def local(
    n_expert, npipe, fwd_state, bwd_state, saved_input, fwd_route, bwd_route, fwd_gate, bwd_gate,
    w_gate, w_up, w_down, norm_gain,
):
    ny = n_expert // NX
    experts = ny // PAIR
    tok, width = fwd_state.shape[1:]
    hid = w_down.shape[1]
    ct = 256
    pad = -(-tok // 16) * 16
    bf, f32 = jnp.bfloat16, jnp.float32
    vmem = pl.BlockSpec(memory_space=pltpu.VMEM)
    hbm = pl.BlockSpec(memory_space=pl.ANY)
    ns = ny // PAIR
    scratch = [
        pltpu.VMEM((NX, width, 2 * hid), bf),
        pltpu.VMEM((NX * hid, width), bf),
        pltpu.VMEM((6 * experts * BLK, width // 2), bf),
        pltpu.VMEM((tok, width), bf),
        pltpu.VMEM((6 * ny * BLK, width // 2), bf),
        pltpu.VMEM((NX, 4 * ny, SLOT, 2 * hid), f32),
        pltpu.VMEM((NX, 2 * ny, SLOT, hid), f32),
        pltpu.VMEM((ny * SLOT, NX * hid), bf),
        pltpu.VMEM((NX, ny * SLOT, 2 * hid), bf),
        pltpu.VMEM((2, ns, BLK, width // 2), f32),
    ]
    scratch += [pltpu.VMEM((4, ns, BLK, width // 2), bf)] * 4
    scratch += [
        pltpu.VMEM((tok, width), f32),
        pltpu.VMEM((pad, width), bf),
        pltpu.VMEM((pad, width), bf),
        pltpu.VMEM((pad, width), bf),
        pltpu.VMEM((pad, width), bf),
    ]
    scratch += [
        pltpu.SemaphoreType.DMA(shape)
        for shape in (
            (3,), (18,), (18,), (6, ns), (6, ns), (6, ns), (6, ns), (4, ns), (4, ns), (4, ns), (4, ns),
            (2,), (2,),
        )
    ]
    fo, bo = pl.pallas_call(
        functools.partial(kernel, ny, npipe, ct),
        out_shape=[jax.ShapeDtypeStruct((tok, width), bf)] * 2,
        in_specs=[vmem] * 8 + [hbm] * 3,
        out_specs=[vmem] * 2,
        scratch_shapes=scratch,
        compiler_params=pltpu.CompilerParams(
            collective_id=0, has_side_effects=True, vmem_limit_bytes=56 << 20
        ),
    )(
        fwd_state[0], bwd_state[0], saved_input[0], fwd_route.reshape(2, tok), bwd_route.reshape(2, tok),
        fwd_gate[0], bwd_gate[0], norm_gain, w_gate[0], w_up[0], w_down[0],
    )
    return fo[None], bo[None]


def solution(mesh):
    placed = (
        P("pipe", "expert", None),
        P("pipe", "expert", None),
        P("pipe", None, "expert", None),
        P("pipe", None, "expert", None),
        P("pipe", None, "expert", None),
        P("pipe", None, "expert"),
        P("pipe", None, "expert"),
        P("pipe", None, "expert"),
        P("pipe", None, "expert"),
        P("pipe", "expert", None),
        P("pipe", None),
    )
    return jax.shard_map(
        functools.partial(local, mesh.shape["expert"], mesh.shape["pipe"]),
        mesh=mesh,
        in_specs=placed,
        out_specs=(P("pipe", "expert", None), P("pipe", "expert", None)),
        check_vma=False,
    )
```

time: 168 us -> 150 us (0.89)
  the two profiles are of different devices: /device:TPU:388 before, /device:TPU:8 now
where the time goes in v3:
time: 150 us
  Pallas kernels  147 us (98%)
  local copies, waits for them, and re-layouts  2.31 us (2%)
    pallas_call x1, Pallas kernels, local(): pl.pallas_call(functools.partial(kernel, ny, npipe, ct), out_shape=[jax.S...  147 us

profile of v3, /device:TPU:8, one launch (start us, length us, event | category | flops | bytes accessed | tf_op | source)
XLA Modules:
  0.0 149.7 jit_solution(13833751174452276968)
XLA Ops:
  0.6 146.7 %shard_map.122 = (bf16[24,3584]{1,0:T(8,128)(2,1)}, bf16[24,3584]{1,0:T(8,128)(2,1)}) custom-call(bf16[24,3584]{1,0:T(8,128)(2,1)} %bitcast.18, bf16[24,3584]{1,0:T(8,128)(2,1)} %bitcast.19, bf16[2,24,3584]{2,1,0:T(8,128)(2,1)} %bitcast.15, s32[2,24]{1,0:T(2,128)} %bitcast.20, s32[2,24]{1,0:T(2,128)} %bitcast.21, f32[2,24]{1,0:T(2,128)} %bitcast.22, ...), custom_call_target="tpu_custom_call" | custom-call | tf_op jit(solution)/shard_map/pallas_call | solution.py:492
  147.3 0.0 copy-start
  147.3 1.6 %copy.15 = bf16[1,24,3584]{2,1,0:T(8,128)(2,1)} copy(bf16[1,24,3584]{2,1,0:T(8,128)(2,1)} %bitcast.17) | data formatting | bytes 344064
  149.0 0.0 copy-done
  149.0 0.7 copy.16
Async XLA Ops:
  147.3 1.6 %copy-start = (bf16[24,3584]{1,0:T(8,128)(2,1)S(1)}, bf16[24,3584]{1,0:T(8,128)(2,1)}, u32[]{:S(2)}) copy-start(bf16[24,3584]{1,0:T(8,128)(2,1)} %get-tuple-element.5) | copy-start | bytes 516100

commit v4 on v3

--- a/solution.py
+++ b/solution.py
@@ -63,8 +63,8 @@
 def kernel(
     ny, npipe, ct,
     fs, bs, sv, fr, br, fg, bg, gain, wg, wu, wd,
-    fo, bo,
-    wgu, wdn, mm, rows_in, dd, gs, dh, hs, ab, po, xs, xr, rs, rr, dn, xf, xb, yf, yb,
+    res,
+    wgu, wdn, mm, rows_in, dd, gs, dh, hs, ab, po, xs, xr, rs, rr, acc, dn, xf, xb, yf, yb,
     l_sem, ws_sem, wr_sem, ds_sem, dr_sem, es_sem, er_sem, cs_sem, cr_sem, rs_sem, rr_sem, ss_sem, sr_sem,
 ):
     width = wd.shape[1]
@@ -129,7 +129,9 @@
         remote(wgu.at[0], wgu.at[1], ws_sem.at[16], wr_sem.at[16], taker),
         remote(wdn.at[pl.ds(0, hid)], wdn.at[pl.ds(hid, hid)], ws_sem.at[17], wr_sem.at[17], taker),
     ]
-    passed = [remote(part(2, i), part(3, i), ws_sem.at[8 + i], wr_sem.at[8 + i], taker) for i in range(8)]
+    passed = [remote(part(2, i), part(3, i), ws_sem.at[8 + i], wr_sem.at[8 + i], taker) for i in range(7)]
+    by_partner = remote(part(1, 7), part(3, 7), ws_sem.at[15], wr_sem.at[15], partner)
+
     far_first = list(range(ns - 1, 0, -1))
 
     def blk(ref, i):
@@ -204,11 +206,11 @@
 
     fill_tokens(0, 0, fs)
     pl.semaphore_wait(barrier, len(peers))
-    scatter(0)
     loads[0].wait()
     loads[1].wait()
+    to_taker[0].start()
+    scatter(0)
     to_partner[0].start()
-    to_taker[0].start()
     fill_grads(2, 0, bs)
     scatter(2)
     b_scale = [fill_saved(1, 0)]
@@ -256,14 +258,13 @@
         passed[i].start()
     for c in to_taker:
         c.wait_recv()
+    by_partner.start()
     into_hidden(1)
-    for i in range(4, 8):
+    for i in range(4, 7):
         to_partner[i].wait_recv()
         passed[i].start()
+    to_partner[7].wait_recv()
     into_hidden(2)
-    for c in passed:
-        c.wait_recv()
-    into_hidden(3)
 
     rows = ny * SLOT
 
@@ -273,47 +274,53 @@
         po[c % 2, :, :, cols] = both[:ns]
         xs[c, :, :, cols] = both[ns:].astype(jnp.bfloat16)
 
-    def out_f(t, at):
-        for q in range(NX):
-            f = gs[q, pl.ds(at * ny, ny)].reshape(rows, 2 * hid)
-            gated, upped = f[:, :hid], f[:, hid:]
-            hidden = gated * jax.nn.sigmoid(gated) * upped
-            hs[:, pl.ds(q * hid, hid)] = hidden.astype(jnp.bfloat16)
-
+    def hidden_f(q, at):
+        f = gs[q, pl.ds(at * ny, ny)].reshape(rows, 2 * hid)
+        gated, upped = f[:, :hid], f[:, hid:]
+        hidden = gated * jax.nn.sigmoid(gated) * upped
+        hs[:, pl.ds(q * hid, hid)] = hidden.astype(jnp.bfloat16)
+
+    def hidden_b(q, t, at):
+        b = gs[q, pl.ds(at * ny, ny)].reshape(rows, 2 * hid)
+        gated, upped = b[:, :hid], b[:, hid:]
+        dhid = dh[q, pl.ds(t * ny, ny)].reshape(rows, hid)
+        s = jax.nn.sigmoid(gated)
+        da = dhid * upped * s * (1.0 + gated * (1.0 - s))
+        db = dhid * gated * s
+        ab[q, :, pl.ds(0, hid)] = da.astype(jnp.bfloat16)
+        ab[q, :, pl.ds(hid, hid)] = db.astype(jnp.bfloat16)
+
+    def part_f(qs, start):
+        units = pl.ds(qs[0] * hid, len(qs) * hid)
+        return dot(hs[:, units], wdn[units, pl.ds(start, ct)])
+
+    def part_b(qs, start):
+        terms = [dot_nt(ab[q], wgu[q, pl.ds(start, ct), :]) for q in qs]
+        return functools.reduce(lambda a, b: a + b, terms)
+
+    def early(kind, product, qs):
         def tile(i, carry):
-            start = pl.multiple_of(i * ct, ct)
-            lo = dot(hs[...], wdn[:, pl.ds(start, ct)])
-            hi = dot(hs[...], wdn[:, pl.ds(pl.multiple_of(half + start, 128), ct)])
-            put_out(2 * t, i, lo, hi)
+            for w in both_halves(i)[1]:
+                acc[kind, :, w] = product(qs, w.start)
             return carry
 
         lax.fori_loop(0, tiles, tile, 0)
-        half_start(2 * t)
-
-    def out_b(t, at):
-        for q in range(NX):
-            b = gs[q, pl.ds(at * ny, ny)].reshape(rows, 2 * hid)
-            gated, upped = b[:, :hid], b[:, hid:]
-            dhid = dh[q, pl.ds(t * ny, ny)].reshape(rows, hid)
-            s = jax.nn.sigmoid(gated)
-            da = dhid * upped * s * (1.0 + gated * (1.0 - s))
-            db = dhid * gated * s
-            ab[q, :, pl.ds(0, hid)] = da.astype(jnp.bfloat16)
-            ab[q, :, pl.ds(hid, hid)] = db.astype(jnp.bfloat16)
-
-        def through(start):
-            b = dot_nt(ab[0], wgu[0, pl.ds(start, ct), :])
-            for q in range(1, NX):
-                b = b + dot_nt(ab[q], wgu[q, pl.ds(start, ct), :])
-            return b
-
+
+    def out(c, product, qs, with_early):
         def tile(i, carry):
-            start = pl.multiple_of(i * ct, ct)
-            put_out(2 * t + 1, i, through(start), through(pl.multiple_of(half + start, 128)))
+            sums = []
+            for w in both_halves(i)[1]:
+                value = product(qs, w.start)
+                sums.append(value + acc[c % 2, :, w] if with_early else value)
+            put_out(c, i, *sums)
             return carry
 
         lax.fori_loop(0, tiles, tile, 0)
-        half_start(2 * t + 1)
+        half_start(c)
+
+    def both_halves(i):
+        start = pl.multiple_of(i * ct, ct)
+        return pl.ds(start, ct), (pl.ds(start, ct), pl.ds(pl.multiple_of(half + start, 128), ct))
 
     def half_copy(c, j):
         return remote(xs.at[c, j], xr.at[c, j], cs_sem.at[c, j], cr_sem.at[c, j], across)
@@ -339,10 +346,6 @@
     jb = lax.broadcasted_iota(jnp.int32, (tok, ns * BLK), 1) // BLK
     step = jnp.where(jb % 2 == 0, jb, -jb) * sg
     expert_of = ((y + step + ny) % ny) // PAIR
-
-    def both_halves(i):
-        start = pl.multiple_of(i * ct, ct)
-        return pl.ds(start, ct), (pl.ds(start, ct), pl.ds(pl.multiple_of(half + start, 128), ct))
 
     def finish_f(t, old, out):
         sel = [pick(routes_f[t], slots_f[t], expert_of, shift) for shift in (0, SLOT)]
@@ -384,8 +387,19 @@
 
         lax.fori_loop(0, tiles, tile2, 0)
 
-    out_f(0, 0)
-    out_b(0, 1)
+    some, last = list(range(NX - 1)), [NX - 1]
+    for q in some:
+        hidden_f(q, 0)
+        hidden_b(q, 0, 1)
+    early(0, part_f, some)
+    early(1, part_b, some)
+    for c in passed + [by_partner]:
+        c.wait_recv()
+    into_hidden(NX - 1)
+    hidden_f(NX - 1, 0)
+    out(0, part_f, last, True)
+    hidden_b(NX - 1, 0, 1)
+    out(1, part_b, last, True)
     back_start(0)
     back_start(1)
     pass_copy(3, 0).start()
@@ -420,19 +434,21 @@
     scatter_end(4)
     for q in range(NX):
         through_up(q, 4, 1, 3)
-    out_f(1, 3)
+        hidden_f(q, 3)
+    out(2, part_f, some + last, False)
     scatter_end(5)
     for q in range(NX):
         through_down(q, 5, 1)
-    out_b(1, 2)
+        hidden_b(q, 1, 2)
+    out(3, part_b, some + last, False)
     back_start(2)
     back_start(3)
     back_wait(2)
-    finish_f(1, f_old, fo)
+    finish_f(1, f_old, res.at[0])
     back_wait(3)
-    finish_b(1, b_old, bo)
-
-    for c in to_partner + to_taker + passed:
+    finish_b(1, b_old, res.at[1])
+
+    for c in to_partner + to_taker + passed + [by_partner]:
         c.wait_send()
     for kind in range(6):
         for j in range(ns):
@@ -476,6 +492,7 @@
     ]
     scratch += [pltpu.VMEM((4, ns, BLK, width // 2), bf)] * 4
     scratch += [
+        pltpu.VMEM((2, ny * SLOT, width), f32),
         pltpu.VMEM((tok, width), f32),
         pltpu.VMEM((pad, width), bf),
         pltpu.VMEM((pad, width), bf),
@@ -489,11 +506,11 @@
             (2,), (2,),
         )
     ]
-    fo, bo = pl.pallas_call(
+    res = pl.pallas_call(
         functools.partial(kernel, ny, npipe, ct),
-        out_shape=[jax.ShapeDtypeStruct((tok, width), bf)] * 2,
+        out_shape=jax.ShapeDtypeStruct((2, tok, width), bf),
         in_specs=[vmem] * 8 + [hbm] * 3,
-        out_specs=[vmem] * 2,
+        out_specs=vmem,
         scratch_shapes=scratch,
         compiler_params=pltpu.CompilerParams(
             collective_id=0, has_side_effects=True, vmem_limit_bytes=56 << 20
@@ -502,7 +519,7 @@
         fwd_state[0], bwd_state[0], saved_input[0], fwd_route.reshape(2, tok), bwd_route.reshape(2, tok),
         fwd_gate[0], bwd_gate[0], norm_gain, w_gate[0], w_up[0], w_down[0],
     )
-    return fo[None], bo[None]
+    return res[0:1], res[1:2]
 
 
 def solution(mesh):

time: 150 us -> 149 us (level)
    unnamed x4 -> x0, local copies, waits for them, and re-layouts: 2.31 us -> none
    slice x0 -> x1, local copies, waits for them, and re-layouts: none -> 1.75 us  [local(): return (res[0:1], res[1:2])]
where the time goes in v4:
time: 149 us
  Pallas kernels  146 us (98%)
  local copies, waits for them, and re-layouts  1.75 us (1%)
    pallas_call x1, Pallas kernels, local(): pl.pallas_call(functools.partial(kernel, ny, npipe, ct), out_shape=jax.Sh...  146 us

profile of v4, /device:TPU:8, one launch (start us, length us, event | category | flops | bytes accessed | tf_op | source)
XLA Modules:
  0.0 148.6 jit_solution(12251279005193153033)
XLA Ops:
  0.6 146.2 %shard_map.122 = bf16[2,24,3584]{2,1,0:T(8,128)(2,1)} custom-call(bf16[24,3584]{1,0:T(8,128)(2,1)} %bitcast.14, bf16[24,3584]{1,0:T(8,128)(2,1)} %bitcast.15, bf16[2,24,3584]{2,1,0:T(8,128)(2,1)} %bitcast.13, s32[2,24]{1,0:T(2,128)} %bitcast.16, s32[2,24]{1,0:T(2,128)} %bitcast.17, f32[2,24]{1,0:T(2,128)} %bitcast.18, f32[2,24]{1,0:T(2,128)} %bitcast.19, ...), custom_call_target="tpu_custom_call" | custom-call | tf_op jit(solution)/shard_map/pallas_call | solution.py:509
  146.8 1.8 %fusion = (bf16[1,24,3584]{2,1,0:T(8,128)(2,1)}, bf16[1,24,3584]{2,1,0:T(8,128)(2,1)}) fusion(bf16[2,24,3584]{2,1,0:T(8,128)(2,1)} %shard_map.122), kind=kLoop, calls=%fused_computation | loop fusion | bytes 688128 | tf_op jit(solution)/shard_map/slice | solution.py:522

commit v5 on v4

--- a/solution.py
+++ b/solution.py
@@ -218,10 +218,11 @@
     loads[2].wait()
     for c in to_partner[1:]:
         c.start()
+    scatter_pass(0)
+    to_taker[1].start()
+    for kind in (2, 1):
+        scatter_pass(kind)
     b_scale.append(fill_saved(3, 1))
-    for kind in (0, 2, 1):
-        scatter_pass(kind)
-    to_taker[1].start()
     for j in far_first:
         send_copy(3, j).start()
     blk(dd, 3 * ny)[...] = blk(mm, 3 * groups + y // PAIR)[...]

time: 149 us -> 149 us (level)
  no operation moved by 1% of the time
where the time goes in v5:
time: 149 us
  Pallas kernels  146 us (98%)
  local copies, waits for them, and re-layouts  1.75 us (1%)
    pallas_call x1, Pallas kernels, local(): pl.pallas_call(functools.partial(kernel, ny, npipe, ct), out_shape=jax.Sh...  146 us

profile of v5, /device:TPU:8, one launch (start us, length us, event | category | flops | bytes accessed | tf_op | source)
XLA Modules:
  0.0 148.6 jit_solution(3702256593996849213)
XLA Ops:
  0.6 146.2 %shard_map.122 = bf16[2,24,3584]{2,1,0:T(8,128)(2,1)} custom-call(bf16[24,3584]{1,0:T(8,128)(2,1)} %bitcast.14, bf16[24,3584]{1,0:T(8,128)(2,1)} %bitcast.15, bf16[2,24,3584]{2,1,0:T(8,128)(2,1)} %bitcast.13, s32[2,24]{1,0:T(2,128)} %bitcast.16, s32[2,24]{1,0:T(2,128)} %bitcast.17, f32[2,24]{1,0:T(2,128)} %bitcast.18, f32[2,24]{1,0:T(2,128)} %bitcast.19, ...), custom_call_target="tpu_custom_call" | custom-call | tf_op jit(solution)/shard_map/pallas_call | solution.py:510
  146.9 1.8 %fusion = (bf16[1,24,3584]{2,1,0:T(8,128)(2,1)}, bf16[1,24,3584]{2,1,0:T(8,128)(2,1)}) fusion(bf16[2,24,3584]{2,1,0:T(8,128)(2,1)} %shard_map.122), kind=kLoop, calls=%fused_computation | loop fusion | bytes 688128 | tf_op jit(solution)/shard_map/slice | solution.py:523
